TPU v7x, 256 devices: a whole 4x4x8 slice. The times are simulated.
256 devices in a mesh: dp: 16 (over y, z_hi, core), seq: 16 (over z_lo, x).
Axes of the slice: x: 4, y: 4, z: 8 (z_hi: 2, z_lo: 4; z = z_hi * 4 + z_lo), core: 2. Of those that a mesh axis runs over, the one named last changes fastest.
Arguments:
- query_nope: bfloat16 [32768, 64, 128], P(('dp', 'seq')), may hold values from -6 to 6
- query_rope: bfloat16 [32768, 4096], P(('dp', 'seq')), may hold values from -8 to 8
- out_grad: bfloat16 [32768, 64, 128], P(('dp', 'seq')), may hold values from -6 to 6
- latent_rows: bfloat16 [32768, 576], P(('dp', 'seq')), may hold values from -6 to 6
- prompt_latent: bfloat16 [16, 128, 576], P('dp', 'seq'), may hold values from -8 to 8
- key_weight: bfloat16 [64, 128, 512], P('seq'), may hold values from -0.5 to 0.5
- value_weight: bfloat16 [64, 128, 512], P('seq'), may hold values from -0.25 to 0.25
- prompt_of: int32 [16, 16], replicated, may hold values from 0 to 15
- prompt_len: int32 [16], replicated, may hold values from 32 to 128, as said below
- response_ids: int32 [256, 128], P(('dp', 'seq')), may hold values from 0 to 3, never falling along the last dimension, each value on 1 to 64 neighbouring positions
Outputs:
- grad_nope: bfloat16 [32768, 64, 128], P(('dp', 'seq'))
- grad_rope: bfloat16 [32768, 4096], P(('dp', 'seq'))
- grad_latent: bfloat16 [32768, 576], P(('dp', 'seq'))
- grad_prompt: float32 [16, 128, 576], P('dp', 'seq')
Inputs may be any that keep to these rules, and one draw needn't show every extreme that they name: `prompt_len`: some prompt has exactly 128 live rows in every draw.
All inputs are finite; a program needn't handle non-finite values.
Results may differ from a plain program's by a relative error of at most 0.015.
Values may be sent and summed in bfloat16 or wider, within the bound.
No kernel may reach another device: no remote copies, remote signals or barrier semaphores. Data moves between devices by JAX's collectives and lax.ppermute only.
A program may use at most 128 MiB of HBM per device.

v0:
```python
import jax
import jax.numpy as jnp
from jax import lax
from jax.sharding import PartitionSpec as P

NOPE = 128
ROPE = 64
LATENT = 512


masked_score = -1e30


def local(
    query_nope,
    query_rope,
    out_grad,
    latent_rows,
    prompt_latent,
    key_weight,
    value_weight,
    prompt_of,
    prompt_len,
    response_ids,
):
    group_idx = lax.axis_index("dp")
    member = lax.axis_index("seq")
    group_count = lax.axis_size("dp")
    my_prompt = prompt_of[group_idx, member]
    column = lax.all_gather(prompt_latent, "dp", axis=0, tiled=True)
    every_prompt = lax.all_gather(column, "seq", axis=1, tiled=True)
    prompt_rows = lax.dynamic_index_in_dim(every_prompt, my_prompt, 0, keepdims=False)
    prompt_total = prompt_rows.shape[0]
    row_count = query_nope.shape[0]
    head_count = query_nope.shape[1]
    score_scale = (NOPE + ROPE) ** (-0.5)
    all_keys = jnp.concatenate([prompt_rows, latent_rows], 0)
    latent_keys = all_keys[:, :LATENT]
    rotary_keys = all_keys[:, LATENT:]
    seg_ids = response_ids[0]
    positions = jnp.arange(row_count)
    prompt_size = prompt_len[my_prompt]
    prompt_ok = jnp.broadcast_to(
        (jnp.arange(prompt_total) < prompt_size)[None, :], (row_count, prompt_total)
    )
    own_ok = (positions[None, :] <= positions[:, None]) & (seg_ids[None, :] == seg_ids[:, None])
    key_mask = jnp.concatenate([prompt_ok, own_ok], 1)
    rope_three = query_rope.reshape(row_count, head_count, ROPE)
    key_piece = lax.all_gather(key_weight, "seq", axis=0, tiled=True)
    value_piece = lax.all_gather(value_weight, "seq", axis=0, tiled=True)
    q_lat = jnp.einsum(
        "thd,hdl->thl", query_nope, key_piece, preferred_element_type=jnp.float32
    ).astype(jnp.bfloat16)
    g_lat = jnp.einsum(
        "thd,hdl->thl", out_grad, value_piece, preferred_element_type=jnp.float32
    ).astype(jnp.bfloat16)
    scores = jnp.einsum("thl,kl->htk", q_lat, latent_keys, preferred_element_type=jnp.float32)
    scores = (
        scores
        + jnp.einsum("thr,kr->htk", rope_three, rotary_keys, preferred_element_type=jnp.float32)
    ) * score_scale
    scores = jnp.where(key_mask[None], scores, masked_score)
    row_max = jnp.max(scores, -1, keepdims=True)
    shifted = jnp.exp(scores - row_max)
    prob_w = shifted / jnp.sum(shifted, -1, keepdims=True)
    dprob = jnp.einsum("thl,kl->htk", g_lat, latent_keys, preferred_element_type=jnp.float32)
    delta = jnp.sum(prob_w * dprob, -1, keepdims=True)
    dscore = (prob_w * (dprob - delta) * score_scale).astype(jnp.bfloat16)
    prob_b = prob_w.astype(jnp.bfloat16)
    dquery = jnp.einsum("htk,kc->thc", dscore, all_keys, preferred_element_type=jnp.float32)
    dq_lat = dquery[..., :LATENT].astype(jnp.bfloat16)
    nope_part = jnp.einsum(
        "thl,hdl->thd", dq_lat, key_piece, preferred_element_type=jnp.float32
    ).astype(jnp.bfloat16)
    rope_grad = dquery[..., LATENT:].astype(jnp.bfloat16)
    full_query = jnp.concatenate([q_lat, rope_three], -1)
    dkey_part = jnp.einsum("htk,thc->kc", dscore, full_query, preferred_element_type=jnp.float32)
    dvalue = jnp.einsum("htk,thl->kl", prob_b, g_lat, preferred_element_type=jnp.float32)
    dkey_sum = dkey_part + jnp.pad(dvalue, ((0, 0), (0, ROPE)))
    grad_nope, rope_out, dkey_sum = (nope_part, rope_grad, dkey_sum)
    grad_latent = dkey_sum[prompt_total:].astype(jnp.bfloat16)
    grad_pre = dkey_sum[:prompt_total]
    one_hot = (jnp.arange(group_count) == my_prompt).astype(jnp.float32)
    placed = one_hot[:, None, None] * grad_pre[None]
    grouped = lax.psum_scatter(placed, "seq", scatter_dimension=1, tiled=True)
    owned = lax.psum_scatter(grouped, "dp", scatter_dimension=0, tiled=True)
    return (grad_nope, rope_out.reshape(row_count, head_count * ROPE), grad_latent, owned)


def solution(mesh):
    return jax.shard_map(
        local,
        mesh=mesh,
        in_specs=(
            P(("dp", "seq"), None, None),
            P(("dp", "seq"), None),
            P(("dp", "seq"), None, None),
            P(("dp", "seq"), None),
            P("dp", "seq", None),
            P("seq", None, None),
            P("seq", None, None),
            P(),
            P(),
            P(("dp", "seq"), None),
        ),
        out_specs=(
            P(("dp", "seq"), None, None),
            P(("dp", "seq"), None),
            P(("dp", "seq"), None),
            P("dp", "seq", None),
        ),
        check_vma=False,
    )
```

profile of v0, /device:TPU:1, one launch (start us, length us, event | category | flops | bytes accessed | tf_op | source)
XLA Modules:
  0.0 547.6 jit_solution(8693354709369289550)
XLA Ops:
  7.2 0.0 copy-start
  7.2 0.0 all-gather.4.cloned.1.call-start
  7.2 37.2 %all_gather.12 = bf16[16,8,576]{2,1,0:T(8,128)(2,1)} all-gather(bf16[1,8,576]{2,1,0:T(8,128)(2,1)} %param.14), channel_id=1, replica_groups=mesh['dp'=16,'seq'=16] {'dp'}, dimensions={0}, use_global_device_ids=true | all-gather | bytes 156672 | tf_op jit(solution)/shard_map/all_gather | solution.py:30
  44.5 0.0 all-gather.4.cloned.1.call-update
  44.5 0.0 all-gather.6.cloned.1.call-start
  44.5 0.7 all-gather.6.cloned.1.call-update
  45.2 0.0 all-gather.8.cloned.1.call-start
  45.3 0.7 all-gather.8.cloned.1.call-update
  46.0 0.0 reduce-scatter.5.cloned.1.call-start
  46.0 1.3 dynamic_slice.10
  48.6 1.1 copy.33
  49.7 1.6 copy.37
  51.9 1.2 dynamic_slice.12
  53.2 0.6 iota_compare_fusion.1
  53.8 0.7 compare_convert_fusion
  54.5 0.8 fusion.39
  55.3 0.1 pad_add_fusion
  55.4 58.8 %all-gather.4.cloned.1.call-done = bf16[16,128,576]{2,1,0:T(8,128)(2,1)} async-done(((bf16[16,8,576]{2,1,0:T(8,128)(2,1)}), bf16[16,128,576]{2,1,0:T(8,128)(2,1)}) %all-gather.4.cloned.1.call-update) | async-done | bytes 2359312 | tf_op jit(solution)/shard_map/all_gather | solution.py:31
  114.2 0.9 dynamic-slice_bitcast_fusion
  115.1 111.0 %all-gather.6.cloned.1.call-done = bf16[64,128,512]{2,1,0:T(8,128)(2,1)} async-done(((bf16[4,128,512]{2,1,0:T(8,128)(2,1)}), bf16[64,128,512]{2,1,0:T(8,128)(2,1)}) %all-gather.6.cloned.1.call-update) | async-done | bytes 8388624 | tf_op jit(solution)/shard_map/all_gather | solution.py:49
  226.1 0.0 copy-done
  226.1 8.3 %convert_bitcast_fusion.1 = bf16[128,64,512]{0,2,1:T(8,128)(2,1)S(1)} fusion(bf16[64,128,512]{2,1,0:T(8,128)(2,1)} %all-gather.6.cloned.1.call-done, bf16[128,64,128]{2,1,0:T(8,128)(2,1)S(1)} %copy-done), kind=kOutput, calls=%fused_computation.20 | convolution fusion | flops 1077936128 | bytes 18874368 | tf_op jit(solution)/shard_map/thd,hdl->thl/dot_general | solution.py:51
  234.4 0.0 copy-start.2
  234.4 3.2 copy-done.2
  237.6 0.0 copy-start.4
  237.7 5.7 %fusion.41 = f32[256,128,64]{1,0,2:T(8,128)} fusion(bf16[128,64,512]{0,2,1:T(8,128)(2,1)S(1)} %convert_bitcast_fusion.1, bf16[128,576]{1,0:T(8,128)(2,1)S(1)} %dynamic-slice_bitcast_fusion, bf16[128,576]{1,0:T(8,128)(2,1)S(1)} %copy.33), kind=kOutput, calls=%fused_computation.47 | convolution fusion | flops 2148007936 | bytes 17072128 | tf_op jit(solution)/shard_map/thl,kl->htk/dot_general | solution.py:57
  243.3 83.8 %all-gather.8.cloned.1.call-done = bf16[64,128,512]{2,1,0:T(8,128)(2,1)} async-done(((bf16[4,128,512]{2,1,0:T(8,128)(2,1)}), bf16[64,128,512]{2,1,0:T(8,128)(2,1)}) %all-gather.8.cloned.1.call-update) | async-done | bytes 8388624 | tf_op jit(solution)/shard_map/all_gather | solution.py:50
  327.1 0.0 copy-done.4
  327.1 8.3 %convolution_convert_fusion = bf16[64,512,128]{2,1,0:T(8,128)(2,1)S(1)} fusion(bf16[64,128,512]{2,1,0:T(8,128)(2,1)} %all-gather.8.cloned.1.call-done, bf16[128,64,128]{2,1,0:T(8,128)(2,1)S(1)} %copy-done.4), kind=kOutput, calls=%fused_computation.21 | convolution fusion | flops 1077936128 | bytes 18874368 | tf_op jit(solution)/shard_map/thd,hdl->thl/dot_general | solution.py:54
  335.5 0.0 copy-start.3
  335.5 5.7 %fusion.13 = f32[256,128,64]{1,0,2:T(8,128)} fusion(bf16[64,512,128]{2,1,0:T(8,128)(2,1)S(1)} %convolution_convert_fusion, bf16[128,576]{1,0:T(8,128)(2,1)S(1)} %dynamic-slice_bitcast_fusion, bf16[128,576]{1,0:T(8,128)(2,1)S(1)} %copy.33), kind=kOutput, calls=%fused_computation.16 | convolution fusion | flops 2148007936 | bytes 17072128 | tf_op jit(solution)/shard_map/thl,kl->htk/dot_general | solution.py:66
  341.2 0.0 copy-done.3
  341.2 7.2 %fusion.52 = (f32[64,128]{1,0:T(8,128)S(1)}, f32[64,128,256]{1,2,0:T(8,128)}) fusion(f32[256,128,64]{1,0,2:T(8,128)} %fusion.41, pred[128,256]{0,1:T(8,128)(4,1)S(1)} %pad_add_fusion, bf16[128,64,64]{0,2,1:T(8,128)(2,1)S(1)} %bitcast.78, bf16[128,576]{1,0:T(8,128)(2,1)S(1)} %dynamic-slice_bitcast_fusion, bf16[128,576]{1,0:T(8,128)(2,1)S(1)} %copy.33), kind=kOutput, calls=%fused_computation.59 | convolution fusion | flops 278987008 | bytes 18186240 | tf_op jit(solution)/shard_map/sub | solution.py:64
  348.4 8.1 %fusion.24 = f32[256,512]{0,1:T(8,128)S(1)} fusion(bf16[64,512,128]{2,1,0:T(8,128)(2,1)} %copy-done.3, f32[64,128,256]{1,2,0:T(8,128)} %get-tuple-element.13, f32[64,128]{1,0:T(8,128)S(1)} %get-tuple-element.12), kind=kOutput, calls=%fused_computation.30 | convolution fusion | flops 2151677952 | bytes 17334272 | tf_op jit(solution)/shard_map/htk,thl->kl/dot_general | solution.py:78
  356.5 15.2 %fusion.29 = f32[256,576]{0,1:T(8,128)S(1)} fusion(bf16[128,64,64]{0,2,1:T(8,128)(2,1)S(1)} %bitcast.79, bf16[128,64,512]{0,2,1:T(8,128)(2,1)} %copy-done.2, f32[256,128,64]{1,0,2:T(8,128)} %fusion.13, f32[256,512]{0,1:T(8,128)S(1)} %fusion.24, f32[64,128,256]{1,2,0:T(8,128)} %get-tuple-element.13, f32[64,128]{1,0:T(8,128)S(1)} %get-tuple-element.12), kind=kOutput, calls=%fused_computation.31 | convolution fusion | flops 2449629440 | bytes 27361280 | tf_op jit(solution)/shard_map/htk,thc->kc/dot_general | solution.py:77
  371.8 0.0 copy-start.5
  371.8 0.2 copy.48
  372.0 2.9 broadcast_multiply_fusion
  374.9 0.0 reduce-scatter.5.cloned.1.call-update
  374.9 0.0 reduce-scatter.7.cloned.1.call-start
  375.0 16.5 %convert_bitcast_fusion = bf16[128,64,576]{0,2,1:T(8,128)(2,1)} fusion(f32[256,128,64]{1,0,2:T(8,128)} %fusion.13, bf16[128,576]{1,0:T(8,128)(2,1)S(1)} %copy.33, bf16[128,576]{1,0:T(8,128)(2,1)S(1)} %dynamic-slice_bitcast_fusion, f32[64,128,256]{1,2,0:T(8,128)} %get-tuple-element.13, f32[64,128]{1,0:T(8,128)S(1)} %get-tuple-element.12), kind=kOutput, calls=%fused_computation.6 | convolution fusion | flops 2435916032 | bytes 26542080 | tf_op jit(solution)/shard_map/htk,kc->thc/dot_general | solution.py:70
  391.4 0.0 copy-done.5
  391.4 67.0 %reduce-scatter.5.cloned.1.call-done = f32[16,8,576]{2,1,0:T(8,128)} async-done(((f32[16,128,576]{2,1,0:T(8,128)}), f32[16,8,576]{2,1,0:T(8,128)}) %reduce-scatter.5.cloned.1.call-update) | async-done | bytes 294928 | tf_op jit(solution)/shard_map/reduce_scatter | solution.py:85
  458.4 0.0 reduce-scatter.7.cloned.1.call-update
  458.5 0.0 slice-start
  458.5 0.0 copy-start.1
  458.5 7.5 %convert_bitcast_fusion.2 = bf16[128,64,128]{2,0,1:T(8,128)(2,1)S(1)} fusion(bf16[64,128,512]{2,1,0:T(8,128)(2,1)} %all-gather.6.cloned.1.call-done, bf16[128,64,576]{0,2,1:T(8,128)(2,1)} %convert_bitcast_fusion), kind=kOutput, calls=%fused_computation.28 | convolution fusion | flops 1074790400 | bytes 18874368 | tf_op jit(solution)/shard_map/thl,hdl->thd/dot_general | solution.py:72
  466.0 1.6 slice.62
  467.7 2.7 copy.49
  470.3 0.0 slice-done
  470.3 1.3 copy.50
  471.6 69.5 %reduce-scatter.7.cloned.1.call-done = f32[1,8,576]{2,1,0:T(8,128)} async-done(((f32[16,8,576]{2,1,0:T(8,128)}), f32[1,8,576]{2,1,0:T(8,128)}) %reduce-scatter.7.cloned.1.call-update) | async-done | bytes 18448
  541.1 0.0 copy-done.1
  (2 shorter events, 0.0 us)
Async XLA Ops:
  7.2 218.9 %copy-start = (bf16[128,64,128]{2,1,0:T(8,128)(2,1)S(1)}, bf16[128,64,128]{2,1,0:T(8,128)(2,1)}, u32[]{:S(2)}) copy-start(bf16[128,64,128]{2,1,0:T(8,128)(2,1)} %param.10) | copy-start | bytes 6291460
  7.2 107.0 %all-gather.4.cloned.1.call-start = ((), (), s32[]{:S(2)}) async-start(), calls=%async_computation.2 | async-start | bytes 2785280 | tf_op jit(solution)/shard_map/all_gather | solution.py:31
  44.5 181.6 %all-gather.6.cloned.1.call-start = ((), (), s32[]{:S(2)}) async-start(), calls=%async_computation.3 | async-start | bytes 8912896 | tf_op jit(solution)/shard_map/all_gather | solution.py:49
  45.2 281.9 %all-gather.8.cloned.1.call-start = ((), (), s32[]{:S(2)}) async-start(), calls=%async_computation.4 | async-start | bytes 8912896 | tf_op jit(solution)/shard_map/all_gather | solution.py:50
  46.0 412.5 %reduce-scatter.5.cloned.1.call-start = ((), (), s32[]{:S(2)}) async-start(), calls=%async_computation.5 | async-start | bytes 5570560 | tf_op jit(solution)/shard_map/reduce_scatter | solution.py:85
  234.4 3.2 copy-start.2
  237.6 89.5 %copy-start.4 = (bf16[128,64,128]{2,1,0:T(8,128)(2,1)S(1)}, bf16[128,64,128]{2,1,0:T(8,128)(2,1)}, u32[]{:S(2)}) copy-start(bf16[128,64,128]{2,1,0:T(8,128)(2,1)} %param.12) | copy-start | bytes 6291460
  335.5 5.7 %copy-start.3 = (bf16[64,512,128]{2,1,0:T(8,128)(2,1)}, bf16[64,512,128]{2,1,0:T(8,128)(2,1)S(1)}, u32[]{:S(2)}) copy-start(bf16[64,512,128]{2,1,0:T(8,128)(2,1)S(1)} %convolution_convert_fusion) | copy-start | bytes 25165828
  371.8 19.6 %copy-start.5 = (f32[256,576]{0,1:T(8,128)}, f32[256,576]{0,1:T(8,128)S(1)}, u32[]{:S(2)}) copy-start(f32[256,576]{0,1:T(8,128)S(1)} %fusion.29) | copy-start | bytes 1769476
  374.9 166.2 %reduce-scatter.7.cloned.1.call-start = ((), (), s32[]{:S(2)}) async-start(), calls=%async_computation.6 | async-start | bytes 348160
  458.5 11.9 %slice-start = ((bf16[128,64,576]{0,2,1:T(8,128)(2,1)}), bf16[128,64,64]{0,2,1:T(8,128)(2,1)S(1)}, s32[]{:S(2)}) async-start(bf16[128,64,576]{0,2,1:T(8,128)(2,1)} %convert_bitcast_fusion), calls=%async_computation.7 | async-start | bytes 2097152 | tf_op jit(solution)/shard_map/slice | solution.py:75
  458.5 82.6 %copy-start.1 = (bf16[128,64,128]{2,1,0:T(8,128)(2,1)S(1)}, bf16[128,64,128]{2,1,0:T(8,128)(2,1)}, u32[]{:S(2)}) copy-start(bf16[128,64,128]{2,1,0:T(8,128)(2,1)} %param.10) | copy-start | bytes 6291460
Sparse Core Ops, SparseCore 0:
  44.6 69.5 all-gather.3
  116.0 110.0 all-gather.5
  227.9 99.1 all-gather.7
  375.0 83.3 reduce-scatter.4
  462.8 78.2 reduce-scatter.6
where the time goes:
time: 549 us; the launch traced here: 548 us
  waiting for transfers between devices  391 us (71%)
  matrix products  82.6 us (15%)
  blocking collectives  37.2 us (7%)
  between operations  15.9 us (3%)
  local copies, waits for them, and re-layouts  15.2 us (3%)
    all_gather x1, waiting for transfers between devices, local(): key_piece = lax.all_gather(key_weight, 'seq', axis=0, tiled=True)  111 us
    all_gather x1, waiting for transfers between devices, local(): value_piece = lax.all_gather(value_weight, 'seq', axis=0, tiled=True)  83.8 us
    unnamed x6, waiting for transfers between devices  70.9 us
    reduce_scatter x1, waiting for transfers between devices, local(): grouped = lax.psum_scatter(placed, 'seq', scatter_dimension=1, tiled=True)  67 us
    all_gather x1, waiting for transfers between devices, local(): every_prompt = lax.all_gather(column, 'seq', axis=1, tiled=True)  58.8 us
    all_gather x1, blocking collectives, local(): column = lax.all_gather(prompt_latent, 'dp', axis=0, tiled=True)  37.2 us
    dot_general x1, matrix products, local(): jnp.einsum('htk,kc->thc', dscore, all_keys, preferred_element_type=jnp.fl...  16.5 us
    dot_general x1, matrix products, local(): jnp.einsum('htk,thc->kc', dscore, full_query, preferred_element_type=jnp....  15.2 us
  transfers between devices with their start and end apart: 5, of which 5 were waited for; matrix products, arithmetic and copies ran while one was open for 9% of the time, Pallas kernels for 0%

commit v1 on v0

v1 whole, which is shorter than its diff:
```python
import functools
import math

import jax
import jax.numpy as jnp
import numpy as np
from jax import lax
from jax.experimental import pallas as pl
from jax.experimental.pallas import tpu as pltpu
from jax.sharding import PartitionSpec as P

NOPE = 128
ROPE = 64
LATENT = 512
WIDTH = LATENT + ROPE
SCALE = (NOPE + ROPE) ** -0.5
LOG2E = math.log2(math.e)
MASKED = -1e30
AXES = ("dp", "seq")
NX, NY, NZ_HI, NZ_LO, NCORE = 4, 4, 2, 4, 2
NZ = NZ_HI * NZ_LO
PPS = 4
F32 = jnp.float32
BF16 = jnp.bfloat16


def place(i):
    x, z_lo = i % NX, i // NX % NZ_LO
    core, z_hi, y = i // 16 % NCORE, i // 32 % NZ_HI, i // 64
    return x, y, z_hi * NZ_LO + z_lo, core


def number(x, y, z, core):
    x, y, z, core = x % NX, y % NY, z % NZ, core % NCORE
    return ((y * NZ_HI + z // NZ_LO) * NCORE + core) * 16 + z % NZ_LO * NX + x


def permute(array, move):
    pairs = []
    for i in range(NX * NY * NZ * NCORE):
        x, y, z, core = place(i)
        dx, dz, dc = move(core)
        pairs.append((i, number(x + dx, y, z + dz, core + dc)))
    return lax.ppermute(array, AXES, pairs)


def swap(array):
    return permute(array, lambda core: (0, 0, 1))


def first_ring(array, step):
    return permute(array, lambda core: (0, step, 0) if core else (step, 0, 0))


def second_ring(array, step):
    return permute(array, lambda core: (step, 0, 0) if core else (0, step, 0))


def nt(a, b):
    return lax.dot_general(a, b, (((1,), (1,)), ((), ())), preferred_element_type=F32)


def tn(a, b):
    return lax.dot_general(a, b, (((0,), (0,)), ((), ())), preferred_element_type=F32)


def nn(a, b):
    return jnp.dot(a, b, preferred_element_type=F32)


def attention_kernel(counts, first, last, pair_ref, prompt_of_ref, prompt_len_ref, *refs):
    sources = len(counts)
    source_refs, refs = refs[:sources], refs[sources:]
    q_refs, refs = refs[:PPS], refs[PPS:]
    g_refs, refs = refs[:PPS], refs[PPS:]
    rope_refs, refs = refs[:PPS], refs[PPS:]
    (prompt_ref, own_ref, own_bias_ref), refs = refs[:3], refs[3:]
    if not first:
        (lat_in, turn_in), refs = refs[:2], refs[4:]
    (first_out, second_out, nope_out, rope_out), refs = refs[:4], refs[4:]
    if last:
        (lat_ref, turn_ref), refs = refs[:2], refs[2:]
    else:
        lat_ref, turn_ref = first_out, second_out
    latent_ref, rot_ref, bias_ref, weights, nope_part, rope_part, sems, weight_sems = refs
    step = pl.program_id(0)
    steps = pl.num_programs(0)
    slot = lax.rem(step, 2)

    tokens, prompts = own_ref.shape[0], prompt_ref.shape[0]

    @pl.when(step == 0)
    def _():
        for begin, rows_ref in ((0, prompt_ref), (prompts, own_ref)):
            here = pl.ds(begin, rows_ref.shape[0])
            latent_ref[here, :] = rows_ref[:, :LATENT]
            rotary = rows_ref[:, LATENT:]
            rot_ref[here, :] = jnp.concatenate([rotary, rotary], 1)
        live = prompt_len_ref[prompt_of_ref[lax.axis_index("dp"), lax.axis_index("seq")]]
        row = lax.broadcasted_iota(jnp.int32, (prompts, 2 * tokens), 0)
        bias_ref[:prompts, :] = jnp.where(row < live, 0.0, MASKED).astype(F32)
        own_bias = own_bias_ref[...]
        bias_ref[prompts:, :] = jnp.concatenate([own_bias, own_bias], 1)
        if first:
            lat_ref[...] = jnp.zeros_like(lat_ref)
            turn_ref[...] = jnp.zeros_like(turn_ref)
        else:
            lat_ref[...] = lat_in[...]
            turn_ref[...] = turn_in[...]

    def fetch(at):
        begin = 0
        for k in range(sources):
            ahead, lane_of = begin // PPS, begin % PPS

            @pl.when(at == ahead)
            def _(k=k, lane_of=lane_of):
                here = weights.at[at % 2, pl.ds(lane_of, counts[k])]
                pltpu.make_async_copy(source_refs[k], here, weight_sems.at[at % 2]).start()

            begin += counts[k]

    @pl.when(step == 0)
    def _():
        fetch(step)

    @pl.when(step + 1 < steps)
    def _():
        fetch(step + 1)

    pltpu.make_async_copy(weights.at[slot], weights.at[slot], weight_sems.at[slot]).wait()

    def copies(at, where):
        out = []
        for p in range(PPS):
            pair = pair_ref[at * PPS + p]
            out.append(pltpu.make_async_copy(nope_part.at[where, p], nope_out.at[pair], sems.at[where, 0, p]))
            lanes = pl.ds(pl.multiple_of(pair * 2 * ROPE, 2 * ROPE), 2 * ROPE)
            out.append(pltpu.make_async_copy(rope_part.at[where, p], rope_out.at[:, lanes], sems.at[where, 1, p]))
        return out

    @pl.when(step >= 2)
    def _():
        for copy in copies(step - 2, slot):
            copy.wait()

    latent = latent_ref[...]
    rot = rot_ref[...]
    bias = bias_ref[...]
    lane = lax.broadcasted_iota(jnp.int32, (tokens, 2 * ROPE), 1) // ROPE
    mine = lane == 0
    none = jnp.zeros((tokens, NOPE), BF16)
    zero = jnp.zeros((tokens, 2 * ROPE), BF16)
    kept = [{} for _ in range(PPS)]

    def project(p):
        up = nt(latent, weights[slot, p].reshape(4 * NOPE, LATENT)).astype(BF16)
        kept[p]["keys"] = jnp.concatenate([up[:, :256], rot], 1)
        kept[p]["values"] = up[:, 256:]

    def compare(p):
        q0, q1 = q_refs[p][0, 0], q_refs[p][0, 1]
        g0, g1 = g_refs[p][0, 0], g_refs[p][0, 1]
        rope = rope_refs[p][...]
        rope0, rope1 = jnp.where(mine, rope, zero), jnp.where(mine, zero, rope)
        kept[p]["queries"] = jnp.concatenate(
            [jnp.concatenate([q0, none, rope0], 1), jnp.concatenate([none, q1, rope1], 1)], 0
        )
        kept[p]["out_grad"] = jnp.concatenate(
            [jnp.concatenate([g0, none], 1), jnp.concatenate([none, g1], 1)], 0
        )
        keys = kept[p]["keys"]
        score0 = nt(jnp.concatenate([keys[:, :128], rot], 1), jnp.concatenate([q0, rope0], 1))
        score1 = nt(keys[:, 128:], jnp.concatenate([q1, rope1], 1))
        kept[p]["score"] = jnp.concatenate([score0, score1], 1)
        kept[p]["dprob"] = nt(kept[p]["values"], kept[p]["out_grad"])

    def soften(p):
        score = kept[p]["score"] * (SCALE * LOG2E) + bias
        dprob = kept[p]["dprob"]
        top = jnp.max(score, 0, keepdims=True)
        e = jnp.exp2(score - top)
        inverse = 1.0 / jnp.sum(e, 0, keepdims=True)
        delta = jnp.sum(e * dprob, 0, keepdims=True) * inverse
        prob = e * inverse
        kept[p]["prob"] = prob.astype(BF16)
        kept[p]["dscore"] = (prob * (dprob - delta) * SCALE).astype(BF16)

    def derive(p):
        keys, dscore = kept[p]["keys"], kept[p]["dscore"]
        dkeys = nn(dscore, kept[p]["queries"])
        dvalues = nn(kept[p]["prob"], kept[p]["out_grad"])
        kept[p]["turn"] = dkeys[:, 256:]
        kept[p]["grads"] = [dkeys[:, :256].astype(BF16), dvalues.astype(BF16)]
        dq0 = tn(dscore[:, :tokens], jnp.concatenate([keys[:, :128], rot], 1))
        dq1 = tn(dscore[:, tokens:], jnp.concatenate([keys[:, 128:256], rot], 1))
        nope_part[slot, p, 0] = dq0[:, :128].astype(BF16)
        nope_part[slot, p, 1] = dq1[:, :128].astype(BF16)
        rope_part[slot, p] = jnp.where(mine, dq0[:, 128:], dq1[:, 128:]).astype(BF16)

    stages = (project, compare, soften, derive)
    for tick in range(PPS + len(stages) - 1):
        for k in range(len(stages)):
            if 0 <= tick - k < PPS:
                stages[k](tick - k)
    turn_ref[...] += sum(kept[p]["turn"] for p in range(PPS))
    lat_ref[...] += nn(jnp.concatenate(sum([kept[p]["grads"] for p in range(PPS)], []), 1), weights[slot].reshape(PPS * 4 * NOPE, LATENT))

    for copy in copies(step, slot):
        copy.start()

    if last:

        @pl.when(step == steps - 1)
        def _():
            prompts = first_out.shape[0]
            turned = turn_ref[:, :ROPE] + turn_ref[:, ROPE:]
            total = jnp.concatenate([lat_ref[...], turned], 1)
            first_out[...] = total[:prompts]
            second_out[...] = total[prompts:].astype(BF16)

    @pl.when(step == steps - 1)
    def _():
        if total_steps(counts) > 1:
            for copy in copies(step - 1, 1 - slot):
                copy.wait()
        for copy in copies(step, slot):
            copy.wait()


def total_steps(counts):
    return sum(counts) // PPS


def attention(sources, scalars, q, g, rope, prompt, own, own_bias, state, last=False):
    counts = tuple(source.shape[0] for source in sources)
    first = state is None
    steps = total_steps(counts)
    tokens = own.shape[0]
    keys = prompt.shape[0] + tokens
    any_spec = pl.BlockSpec(memory_space=pl.ANY)

    head_specs = [
        pl.BlockSpec((1, 2, tokens, NOPE), lambda i, pair, *_, p=p: (pair[i * PPS + p], 0, 0, 0))
        for p in range(PPS)
    ]
    rope_specs = [
        pl.BlockSpec((tokens, 2 * ROPE), lambda i, pair, *_, p=p: (0, pair[i * PPS + p])) for p in range(PPS)
    ]

    def whole(shape):
        return pl.BlockSpec(shape, lambda i, *_: (0,) * len(shape))

    in_specs = [any_spec] * len(sources) + head_specs * 2 + rope_specs
    in_specs += [whole(prompt.shape), whole(own.shape), whole(own_bias.shape)]
    operands = list(sources)
    operands += [q] * PPS + [g] * PPS + [rope] * PPS + [prompt, own, own_bias]
    aliases = {}
    if not first:
        operands += list(state)
        in_specs += [whole((keys, LATENT)), whole((keys, 2 * ROPE)), any_spec, any_spec]
        aliases = {len(scalars) + len(operands) - 2: 2, len(scalars) + len(operands) - 1: 3}
    sums = (jax.ShapeDtypeStruct((keys, LATENT), F32), jax.ShapeDtypeStruct((keys, 2 * ROPE), F32))
    sum_scratch = []
    if last:
        sum_scratch = [pltpu.VMEM(s.shape, F32) for s in sums]
        sums = (jax.ShapeDtypeStruct((keys - tokens, WIDTH), F32), jax.ShapeDtypeStruct((tokens, WIDTH), BF16))
    return pl.pallas_call(
        functools.partial(attention_kernel, counts, first, last),
        out_shape=(
            *sums,
            jax.ShapeDtypeStruct(q.shape, BF16),
            jax.ShapeDtypeStruct(rope.shape, BF16),
        ),
        grid_spec=pltpu.PrefetchScalarGridSpec(
            num_scalar_prefetch=len(scalars),
            grid=(steps,),
            in_specs=in_specs,
            out_specs=(whole(sums[0].shape), whole(sums[1].shape), any_spec, any_spec),
            scratch_shapes=sum_scratch
            + [
                pltpu.VMEM((keys, LATENT), BF16),
                pltpu.VMEM((keys, 2 * ROPE), BF16),
                pltpu.VMEM((keys, 2 * tokens), F32),
                pltpu.VMEM((2, PPS, 2, 2, NOPE, LATENT), BF16),
                pltpu.VMEM((2, PPS, 2, tokens, NOPE), BF16),
                pltpu.VMEM((2, PPS, tokens, 2 * ROPE), BF16),
                pltpu.SemaphoreType.DMA((2, 2, PPS)),
                pltpu.SemaphoreType.DMA((2,)),
            ],
        ),
        input_output_aliases=aliases,
        compiler_params=pltpu.CompilerParams(vmem_limit_bytes=48 * 1024 * 1024),
        name="attention",
    )(*scalars, *operands)


def halves_kernel(low_in, high_in, _, low, high):
    low[...] = low_in[...]
    high[...] = high_in[...]


def halves(low, high, before):
    n, *rest = low.shape
    n //= 2

    def block(begin):
        return pl.BlockSpec((1, *rest), lambda i: (begin + i,) + (0,) * len(rest))

    shape = jax.ShapeDtypeStruct((n, *rest), low.dtype)
    return pl.pallas_call(
        halves_kernel,
        out_shape=(shape, shape),
        grid=(n,),
        in_specs=[block(0), block(n), pl.BlockSpec(memory_space=pl.ANY)],
        out_specs=[block(0), block(0)],
        name="halves",
    )(low, high, before)


def small_call(kernel, prompt_of, rows, dtype, scratch, name):
    block = pl.BlockSpec(rows.shape, lambda i, *_: (0, 0, 0))
    return pl.pallas_call(
        kernel,
        out_shape=jax.ShapeDtypeStruct(rows.shape, dtype),
        grid_spec=pltpu.PrefetchScalarGridSpec(
            num_scalar_prefetch=1, grid=(1,), in_specs=[block], out_specs=block, scratch_shapes=scratch
        ),
        name=name,
    )(prompt_of, rows)


def select_kernel(prompt_ref, rows_ref, out_ref):
    group = lax.axis_index("dp")
    for m in range(rows_ref.shape[0]):
        out_ref[m] = rows_ref[prompt_ref[group, m]]


def select(prompt_of, rows):
    return small_call(select_kernel, prompt_of, rows, rows.dtype, [], "select")


def collect_kernel(prompt_ref, parts_ref, out_ref, sums):
    group = lax.axis_index("dp")
    sums[...] = jnp.zeros_like(sums)
    for m in range(parts_ref.shape[0]):
        sums[prompt_ref[group, m]] += parts_ref[m]
    out_ref[...] = sums[...].astype(out_ref.dtype)


def collect(prompt_of, parts):
    return small_call(collect_kernel, prompt_of, parts, BF16, [pltpu.VMEM(parts.shape, F32)], "collect")


def local(
    query_nope,
    query_rope,
    out_grad,
    latent_rows,
    prompt_latent,
    key_weight,
    value_weight,
    prompt_of,
    prompt_len,
    response_ids,
):
    dp, seq = lax.axis_index("dp"), lax.axis_index("seq")
    members = lax.axis_size("seq")
    core = dp % NCORE
    z_lo, x = seq // NX, seq % NX
    tokens, heads = query_nope.shape[:2]
    rows = prompt_latent.shape[1]
    prompts = members * rows

    with jax.named_scope("weights_first_ring"):
        both = jnp.stack([key_weight.reshape(2, 2, NOPE, LATENT), value_weight.reshape(2, 2, NOPE, LATENT)], 1)
        here = lax.dynamic_index_in_dim(both, core, 0, keepdims=False)
        before, after = first_ring(here, 1), first_ring(here, -1)
        opposite = jnp.stack([first_ring(here[0], 2), first_ring(here[1], -2)])

    with jax.named_scope("prompt_gather"):
        copies = jnp.broadcast_to(prompt_latent, (members, rows, WIDTH))
        column = lax.all_to_all(copies, "dp", 0, 0, tiled=True)

    with jax.named_scope("weights_second_ring"):
        near = jnp.stack([here, before, after, opposite])
        near, column = lax.optimization_barrier((near, column))
        middle = [second_ring(near, 1), second_ring(near, -1)]
        near_peer = swap(near)

    with jax.named_scope("prompt_exchange"):
        prompt_rows = lax.all_to_all(select(prompt_of, column), "seq", 0, 0, tiled=True).reshape(prompts, WIDTH)

    with jax.named_scope("pair_numbers"):
        order = (0, -1, 1, 2)

        def numbers(side, *blocks):
            table = np.array([(a, far) for far, nears in blocks for a in nears], np.int32)
            kind = core ^ side
            dx = jnp.where(kind == 0, table[:, 0], table[:, 1])
            dz = jnp.where(kind == 0, table[:, 1], table[:, 0])
            return (((z_lo + dz) & 3) * NX + ((x + dx) & 3)) * 2 + kind

        first_pairs = jnp.concatenate([numbers(0, (0, order)), numbers(1, (0, order)), numbers(0, (-1, order), (1, order))])
        peer_pairs = numbers(1, (-1, order), (1, order))
        far_pairs = jnp.concatenate([numbers(side, (2, order[:2]), (2, order[2:])) for side in range(2)])

    q = query_nope.reshape(tokens, heads // 2, 2, NOPE).transpose(1, 2, 0, 3)
    g = out_grad.reshape(tokens, heads // 2, 2, NOPE).transpose(1, 2, 0, 3)
    ids = response_ids[0]
    t = jnp.arange(tokens)
    own_ok = (t[:, None] <= t[None, :]) & (ids[:, None] == ids[None, :])
    own_bias = jnp.where(own_ok, 0.0, MASKED).astype(F32)

    def work(sources, pairs, state, last=False):
        scalars = (pairs, prompt_of, prompt_len)
        return attention(sources, scalars, q, g, query_rope, prompt_rows, latent_rows, own_bias, state, last)

    with jax.named_scope("weights_opposite"):
        *middle, low, high = lax.optimization_barrier((*middle, *halves(*middle, prompt_rows)))
        far = [second_ring(low, 1), second_ring(high, -1)]
        middle_peer = [swap(w) for w in middle]
    state = work([near, near_peer, *middle], first_pairs, None)
    *far, turn = lax.optimization_barrier((*far, state[1]))
    state = (state[0], turn, *state[2:])
    far_peer = [swap(w) for w in far]
    state = work(middle_peer, peer_pairs, state)
    prompt_part, grad_latent, grad_nope, grad_rope = work([*far, *far_peer], far_pairs, state, last=True)

    with jax.named_scope("prompt_return"):
        parts = lax.all_to_all(prompt_part.reshape(members, rows, WIDTH), "seq", 0, 0, tiled=True)
        sums = lax.all_to_all(collect(prompt_of, parts), "dp", 0, 0, tiled=True)
        owned = jnp.sum(sums.astype(F32), 0, keepdims=True)

    grad_nope = grad_nope.transpose(2, 0, 1, 3).reshape(tokens, heads, NOPE)
    return grad_nope, grad_rope, grad_latent, owned


def solution(mesh):
    return jax.shard_map(
        local,
        mesh=mesh,
        in_specs=(
            P(AXES, None, None),
            P(AXES, None),
            P(AXES, None, None),
            P(AXES, None),
            P("dp", "seq", None),
            P("seq", None, None),
            P("seq", None, None),
            P(),
            P(),
            P(AXES, None),
        ),
        out_specs=(
            P(AXES, None, None),
            P(AXES, None),
            P(AXES, None),
            P("dp", "seq", None),
        ),
        check_vma=False,
    )
```

time: 549 us -> 155 us (0.28)
  waiting for transfers between devices: 391 us -> 14.2 us
  matrix products: 82.6 us -> 0 us
  Pallas kernels: 0 us -> 41.9 us
  starting transfers between devices: 0.2 us -> 39.9 us
  between operations: 15.9 us -> 0.93 us
    all_gather x3 -> x0, waiting for transfers between devices: 254 us -> none  [the longest x1 111 us: local(): key_piece = lax.all_gather(key_weight, 'seq', axis=0, tiled=True)]
    dot_general x8 -> x0, matrix products: 75.4 us -> none  [the longest x1 16.5 us: local(): jnp.einsum('htk,kc->thc', dscore, all_keys, preferred_element_type=jnp.fl...]
    unnamed x6 -> x0, waiting for transfers between devices: 70.9 us -> none
    reduce_scatter x1 -> x0, waiting for transfers between devices: 67 us -> none  [local(): grouped = lax.psum_scatter(placed, 'seq', scatter_dimension=1, tiled=True)]
    pallas_call x0 -> x6, Pallas kernels: none -> 41.9 us  [the longest x3 34.4 us: attention(): pl.pallas_call(functools.partial(attention_kernel, counts, first, last),...]
    all_gather x1 -> x0, blocking collectives: 37.2 us -> none  [local(): column = lax.all_gather(prompt_latent, 'dp', axis=0, tiled=True)]
    all_to_all x0 -> x2, blocking collectives: none -> 35.8 us  [the longest x1 21.3 us: local(): lax.all_to_all(select(prompt_of, column), 'seq', 0, 0, tiled=True)]
    ppermute x0 -> x13, starting transfers between devices: none -> 24.8 us  [permute(): return lax.ppermute(array, AXES, pairs)]
  transfers between devices with their start and end apart: 5 -> 15, of which waited for: 5 -> 2; matrix products, arithmetic and copies ran while one was open for 9% -> 10% of each run, Pallas kernels for 0% -> 20%
where the time goes in v1:
time: 155 us; the launch traced here: 154 us
  Pallas kernels  41.9 us (27%)
  starting transfers between devices  39.9 us (26%)
  blocking collectives  35.8 us (23%)
  local copies, waits for them, and re-layouts  18 us (12%)
  waiting for transfers between devices  14.2 us (9%)
  other arithmetic  3.62 us (2%)
    pallas_call x3, Pallas kernels, attention(): pl.pallas_call(functools.partial(attention_kernel, counts, first, last),...  34.4 us
    ppermute x13, starting transfers between devices, permute(): return lax.ppermute(array, AXES, pairs)  24.8 us
    all_to_all x1, blocking collectives, local(): lax.all_to_all(select(prompt_of, column), 'seq', 0, 0, tiled=True)  21.3 us
    unnamed x33, local copies, waits for them, and re-layouts  17.3 us
    all_to_all x1, blocking collectives, local(): lax.all_to_all(prompt_part.reshape(members, rows, WIDTH), 'seq', 0, 0, ti...  14.4 us
    all_to_all x1, starting transfers between devices, local(): column = lax.all_to_all(copies, 'dp', 0, 0, tiled=True)  9.31 us
    all_to_all x1, waiting for transfers between devices, local(): column = lax.all_to_all(copies, 'dp', 0, 0, tiled=True)  8.76 us
    all_to_all x1, starting transfers between devices, local(): sums = lax.all_to_all(collect(prompt_of, parts), 'dp', 0, 0, tiled=True)  5.79 us
  transfers between devices with their start and end apart: 15, of which 2 were waited for; matrix products, arithmetic and copies ran while one was open for 10% of the time, Pallas kernels for 20%

profile of v1, /device:TPU:1, one launch (start us, length us, event | category | flops | bytes accessed | tf_op | source)
XLA Modules:
  0.0 154.3 jit_solution(13371774902798750141)
XLA Ops:
  0.6 0.0 copy-start.9
  0.7 1.1 fusion
  1.7 2.5 %collective-permute-start = (bf16[2,2,128,512]{3,2,1,0:T(8,128)(2,1)S(1)}, bf16[2,2,128,512]{3,2,1,0:T(8,128)(2,1)S(1)}, u32[]{:S(2)}, u32[]{:S(2)}) collective-permute-start(bf16[2,2,128,512]{3,2,1,0:T(8,128)(2,1)S(1)} %bitcast.57), channel_id=1, source_target_pairs={{0,1},{1,2},{2,3},{3,0},{4,5},{5,6},{6,7},{7,4},{8,9},{9,10},{10,1... | collective-permute-start | bytes 1572872 | tf_op jit(solution)/shard_map/weights_first_ring/ppermute | solution.py:44
  4.3 4.0 %collective-permute-start.1 = (bf16[2,2,128,512]{3,2,1,0:T(8,128)(2,1)S(1)}, bf16[2,2,128,512]{3,2,1,0:T(8,128)(2,1)S(1)}, u32[]{:S(2)}, u32[]{:S(2)}) collective-permute-start(bf16[2,2,128,512]{3,2,1,0:T(8,128)(2,1)S(1)} %bitcast.58), channel_id=1, source_target_pairs={{0,3},{1,0},{2,1},{3,2},{4,7},{5,4},{6,5},{7,6},{8,11},{9,8},{10,9... | collective-permute-start | bytes 1572872 | tf_op jit(solution)/shard_map/weights_first_ring/ppermute | solution.py:44
  8.4 0.1 collective-permute-start.2
  8.4 3.6 %collective-permute-start.3 = (bf16[2,128,512]{2,1,0:T(8,128)(2,1)S(1)}, bf16[2,128,512]{2,1,0:T(8,128)(2,1)S(1)}, u32[]{:S(2)}, u32[]{:S(2)}) collective-permute-start(bf16[2,128,512]{2,1,0:T(8,128)(2,1)S(1)} %get-tuple-element.55), channel_id=1, source_target_pairs={{0,2},{1,3},{2,0},{3,1},{4,6},{5,7},{6,4},{7,5},{8,10},{9,11},{10,... | collective-permute-start | bytes 786440 | tf_op jit(solution)/shard_map/weights_first_ring/ppermute | solution.py:44
  12.0 0.7 broadcast_in_dim.21
  12.7 9.3 %all-to-all-start = ((bf16[16,8,576]{2,1,0:T(8,128)(2,1)}), bf16[16,8,576]{2,1,0:T(8,128)(2,1)S(1)}, u32[]{:S(2)}, u32[]{:S(2)}) async-start(bf16[16,8,576]{2,1,0:T(8,128)(2,1)} %broadcast_in_dim.21), calls=%async_computation | async-start | bytes 327680 | tf_op jit(solution)/shard_map/prompt_gather/all_to_all | solution.py:383
  22.0 0.0 collective-permute-done.2
  22.0 0.0 collective-permute-done.3
  22.0 0.1 maximum_bitcast_fusion
  22.1 0.0 collective-permute-done
  22.1 0.0 collective-permute-done.1
  22.1 1.6 %pad_maximum_fusion.refs_0_ = bf16[4,2,2,128,512]{4,3,2,1,0:T(8,128)(2,1)} fusion(bf16[1,2,2,128,512]{4,3,2,1,0:T(8,128)(2,1)S(1)} %maximum_bitcast_fusion, bf16[1,2,2,128,512]{4,3,2,1,0:T(8,128)(2,1)S(1)} %bitcast.62, bf16[1,2,2,128,512]{4,3,2,1,0:T(8,128)(2,1)S(1)} %bitcast.61, bf16[1,2,2,128,512]{4,3,2,1,0:T(8,128)(2,1)S(1)} %fusion), kind=kLoop, calls=%fused_computation | loop fusion | flops 3145728 | bytes 4194304 | tf_op jit(solution)/shard_map/weights_second_ring/stack | solution.py:386
  23.7 8.8 %all-to-all-done.rows_ref = bf16[16,8,576]{2,1,0:T(8,128)(2,1)S(1)} async-done(((bf16[16,8,576]{2,1,0:T(8,128)(2,1)}), bf16[16,8,576]{2,1,0:T(8,128)(2,1)S(1)}, u32[]{:S(2)}, u32[]{:S(2)}) %all-to-all-start) | async-done | bytes 147488 | tf_op jit(solution)/shard_map/prompt_gather/all_to_all | solution.py:383
  32.4 0.1 collective-permute-start.4
  32.6 2.5 %collective-permute-start.5 = (bf16[4,2,2,128,512]{4,3,2,1,0:T(8,128)(2,1)}, bf16[4,2,2,128,512]{4,3,2,1,0:T(8,128)(2,1)}, u32[]{:S(2)}, u32[]{:S(2)}) collective-permute-start(bf16[4,2,2,128,512]{4,3,2,1,0:T(8,128)(2,1)} %pad_maximum_fusion.refs_0_), channel_id=1, source_target_pairs={{0,44},{1,45},{2,46},{3,47},{4,0},{5,1},{6,2},{7,3},{8,4},{9,5},{1... | collective-permute-start | bytes 6291464 | tf_op jit(solution)/shard_map/weights_second_ring/ppermute | solution.py:44
  35.1 1.3 collective-permute-start.8
  36.4 0.0 copy-done.8
  36.4 2.4 %select.9 = bf16[16,8,576]{2,1,0:T(8,128)(2,1)} custom-call(s32[16,16]{1,0:T(8,128)} %prompt_ref.3, bf16[16,8,576]{2,1,0:T(8,128)(2,1)} %copy-done.8), custom_call_target="tpu_custom_call" | custom-call | tf_op jit(solution)/shard_map/prompt_exchange/select/pallas_call | solution.py:323
  38.8 21.3 %all_to_all.20 = bf16[16,8,576]{2,1,0:T(8,128)(2,1)} all-to-all(bf16[16,8,576]{2,1,0:T(8,128)(2,1)} %select.9), channel_id=1, replica_groups=mesh['dp'=16,'seq'=16] {'seq'}, dimensions={0} | all-to-all | bytes 294912 | tf_op jit(solution)/shard_map/prompt_exchange/all_to_all | solution.py:392
  60.1 0.0 collective-permute-done.4.low_in.refs_2_
  60.1 0.0 collective-permute-done.5.high_in.refs_3_
  60.1 1.4 copy-done.5
  61.5 2.6 %halves.1 = (bf16[2,2,2,128,512]{4,3,2,1,0:T(8,128)(2,1)}, bf16[2,2,2,128,512]{4,3,2,1,0:T(8,128)(2,1)}) custom-call(bf16[4,2,2,128,512]{4,3,2,1,0:T(8,128)(2,1)} %copy-done.5, bf16[4,2,2,128,512]{4,3,2,1,0:T(8,128)(2,1)} %collective-permute-done.5.high_in.refs_3_, bf16[128,576]{1,0:T(8,128)(2,1)} %bitcast.28), custom_call_target="tpu_custom_call" | custom-call | tf_op jit(solution)/shard_map/weights_opposite/halves/pallas_call | solution.py:311
  64.1 0.5 collective-permute-start.6
  64.6 7.0 %collective-permute-start.11 = (bf16[4,2,2,128,512]{4,3,2,1,0:T(8,128)(2,1)}, bf16[4,2,2,128,512]{4,3,2,1,0:T(8,128)(2,1)S(1)}, u32[]{:S(2)}, u32[]{:S(2)}) collective-permute-start(bf16[4,2,2,128,512]{4,3,2,1,0:T(8,128)(2,1)} %copy-done.5), channel_id=1, source_target_pairs={{0,16},{1,17},{2,18},{3,19},{4,20},{5,21},{6,22},{7,23},{8,24},{9,... | collective-permute-start | bytes 6291464 | tf_op jit(solution)/shard_map/weights_opposite/ppermute | solution.py:44
  71.6 0.0 collective-permute-start.12
  71.6 1.5 collective-permute-start.7
  73.1 4.4 %copy.42 = bf16[128,64,128]{2,0,1:T(8,128)(2,1)} copy(bf16[128,64,128]{2,1,0:T(8,128)(2,1)} %param.34) | data formatting | bytes 4194304 | tf_op args[0]
  77.5 0.0 copy-done.7
  77.5 0.0 copy-start.10
  77.5 0.0 copy-start
  77.5 0.0 copy-start.3
  77.6 0.0 copy-start.4
  77.6 2.7 %copy.43 = bf16[128,64,128]{2,0,1:T(8,128)(2,1)} copy(bf16[128,64,128]{2,1,0:T(8,128)(2,1)S(1)} %copy-done.7) | data formatting | bytes 4194304 | tf_op args[2]
  80.3 1.1 copy.44.refs_17_.refs_15_
  81.4 0.0 copy-done.11
  81.4 0.0 copy-done.12
  81.4 0.1 pad_add_fusion.1.pair_ref
  81.5 0.1 fusion.2.refs_18_.refs_16_
  81.6 0.0 collective-permute-done.8.refs_1_
  81.7 15.7 %attention.3 = (f32[256,512]{1,0:T(8,128)S(1)}, f32[256,128]{1,0:T(8,128)S(1)}, bf16[32,2,128,128]{3,2,1,0:T(8,128)(2,1)S(1)}, bf16[128,4096]{1,0:T(8,128)(2,1)}) custom-call(s32[16]{0:T(128)S(1)} %pad_add_fusion.1.pair_ref, s32[16,16]{1,0:T(8,128)S(1)} %copy-done.3, s32[16]{0:T(128)S(1)} %copy-done.4, bf16[4,2,2,128,512]{4,3,2,1,0:T(8,128)(2,1)} %pad_maximum_fusion.refs_0_, ...), custom_call_target="tpu_custom_call" | custom-call | tf_op jit(solution)/shard_map/attention/pallas_call | solution.py:268
  97.4 0.0 collective-permute-done.6.refs_0_
  97.4 0.0 collective-permute-done.7.refs_1_
  97.4 1.5 collective-permute-start.10
  98.9 0.1 collective-permute-start.9
  99.0 0.1 pad_add_fusion.pair_ref
  99.1 0.0 collective-permute-done.11.refs_0_
  99.1 0.0 collective-permute-done.12.refs_1_
  99.1 1.3 copy-done.6
  100.4 9.7 %attention.4 = (f32[256,512]{1,0:T(8,128)S(1)}, f32[256,128]{1,0:T(8,128)S(1)}, bf16[32,2,128,128]{3,2,1,0:T(8,128)(2,1)S(1)}, bf16[128,4096]{1,0:T(8,128)(2,1)}) custom-call(s32[8]{0:T(128)S(1)} %get-tuple-element.56.pair_ref, s32[16,16]{1,0:T(8,128)S(1)} %copy-done.3, s32[16]{0:T(128)S(1)} %copy-done.4, ...), custom_call_target="tpu_custom_call", output_to_operand_aliasing={{2}: (22, {}), {3}: (23, {})} | custom-call | tf_op jit(solution)/shard_map/attention/pallas_call | solution.py:268
  110.2 0.0 copy-start.1
  110.2 1.3 copy-done.1
  111.5 0.0 collective-permute-done.10.refs_3_
  111.5 0.0 collective-permute-done.9.refs_2_
  111.5 8.9 %attention.5 = (f32[128,576]{1,0:T(8,128)S(1)}, bf16[128,576]{1,0:T(8,128)(2,1)S(1)}, bf16[32,2,128,128]{3,2,1,0:T(8,128)(2,1)}, bf16[128,4096]{1,0:T(8,128)(2,1)}) custom-call(s32[8]{0:T(128)S(1)} %pad_add_fusion.pair_ref, s32[16,16]{1,0:T(8,128)S(1)} %copy-done.3, s32[16]{0:T(128)S(1)} %copy-done.4, ...), custom_call_target="tpu_custom_call", output_to_operand_aliasing={{2}: (24, {}), {3}: (25, {})} | custom-call | tf_op jit(solution)/shard_map/attention/pallas_call | solution.py:268
  120.5 14.4 %all_to_all.21.parts_ref = f32[16,8,576]{2,1,0:T(8,128)} all-to-all(f32[16,8,576]{2,1,0:T(8,128)S(1)} %bitcast.32), channel_id=1, replica_groups=mesh['dp'=16,'seq'=16] {'seq'}, dimensions={0} | all-to-all | bytes 589824 | tf_op jit(solution)/shard_map/prompt_return/all_to_all | solution.py:431
  134.9 2.5 %collect.1 = bf16[16,8,576]{2,1,0:T(8,128)(2,1)} custom-call(s32[16,16]{1,0:T(8,128)} %prompt_ref.3, f32[16,8,576]{2,1,0:T(8,128)} %all_to_all.21.parts_ref), custom_call_target="tpu_custom_call" | custom-call | tf_op jit(solution)/shard_map/prompt_return/collect/pallas_call | solution.py:323
  137.4 5.8 %all-to-all-start.3 = ((bf16[16,8,576]{2,1,0:T(8,128)(2,1)}), bf16[16,8,576]{2,1,0:T(8,128)(2,1)S(1)}, u32[]{:S(2)}, u32[]{:S(2)}) async-start(bf16[16,8,576]{2,1,0:T(8,128)(2,1)} %collect.1), calls=%async_computation.3 | async-start | bytes 327680 | tf_op jit(solution)/shard_map/prompt_return/all_to_all | solution.py:432
  143.2 4.3 %copy.47 = bf16[128,64,128]{2,1,0:T(8,128)(2,1)} copy(bf16[128,64,128]{2,0,1:T(8,128)(2,1)} %bitcast.27) | data formatting | bytes 4194304
  147.5 0.8 copy.48
  148.2 5.4 %all-to-all-done.3 = bf16[16,8,576]{2,1,0:T(8,128)(2,1)S(1)} async-done(((bf16[16,8,576]{2,1,0:T(8,128)(2,1)}), bf16[16,8,576]{2,1,0:T(8,128)(2,1)S(1)}, u32[]{:S(2)}, u32[]{:S(2)}) %all-to-all-start.3) | async-done | bytes 147488 | tf_op jit(solution)/shard_map/prompt_return/all_to_all | solution.py:432
  153.6 0.6 convert_reduce_fusion
  (18 shorter events, 0.1 us)
Async XLA Ops:
  0.6 11.4 %copy-start.9 = (bf16[1,8,576]{2,1,0:T(8,128)(2,1)S(1)}, bf16[1,8,576]{2,1,0:T(8,128)(2,1)}, u32[]{:S(2)}) copy-start(bf16[1,8,576]{2,1,0:T(8,128)(2,1)} %param.38) | copy-start | bytes 27652
  1.7 20.3 %collective-permute-start = (bf16[2,2,128,512]{3,2,1,0:T(8,128)(2,1)S(1)}, bf16[2,2,128,512]{3,2,1,0:T(8,128)(2,1)S(1)}, u32[]{:S(2)}, u32[]{:S(2)}) collective-permute-start(bf16[2,2,128,512]{3,2,1,0:T(8,128)(2,1)S(1)} %bitcast.57), channel_id=1, source_target_pairs={{0,1},{1,2},{2,3},{3,0},{4,5},{5,6},{6,7},{7,4},{8,9},{9,10},{10,1... | collective-permute-start | bytes 1572872 | tf_op jit(solution)/shard_map/weights_first_ring/ppermute | solution.py:44
  4.3 17.8 %collective-permute-start.1 = (bf16[2,2,128,512]{3,2,1,0:T(8,128)(2,1)S(1)}, bf16[2,2,128,512]{3,2,1,0:T(8,128)(2,1)S(1)}, u32[]{:S(2)}, u32[]{:S(2)}) collective-permute-start(bf16[2,2,128,512]{3,2,1,0:T(8,128)(2,1)S(1)} %bitcast.58), channel_id=1, source_target_pairs={{0,3},{1,0},{2,1},{3,2},{4,7},{5,4},{6,5},{7,6},{8,11},{9,8},{10,9... | collective-permute-start | bytes 1572872 | tf_op jit(solution)/shard_map/weights_first_ring/ppermute | solution.py:44
  8.4 13.6 %collective-permute-start.2 = (bf16[2,128,512]{2,1,0:T(8,128)(2,1)S(1)}, bf16[2,128,512]{2,1,0:T(8,128)(2,1)S(1)}, u32[]{:S(2)}, u32[]{:S(2)}) collective-permute-start(bf16[2,128,512]{2,1,0:T(8,128)(2,1)S(1)} %get-tuple-element.54), channel_id=1, source_target_pairs={{0,2},{1,3},{2,0},{3,1},{4,6},{5,7},{6,4},{7,5},{8,10},{9,11},{10,... | collective-permute-start | bytes 786440 | tf_op jit(solution)/shard_map/weights_first_ring/ppermute | solution.py:44
  8.4 13.6 %collective-permute-start.3 = (bf16[2,128,512]{2,1,0:T(8,128)(2,1)S(1)}, bf16[2,128,512]{2,1,0:T(8,128)(2,1)S(1)}, u32[]{:S(2)}, u32[]{:S(2)}) collective-permute-start(bf16[2,128,512]{2,1,0:T(8,128)(2,1)S(1)} %get-tuple-element.55), channel_id=1, source_target_pairs={{0,2},{1,3},{2,0},{3,1},{4,6},{5,7},{6,4},{7,5},{8,10},{9,11},{10,... | collective-permute-start | bytes 786440 | tf_op jit(solution)/shard_map/weights_first_ring/ppermute | solution.py:44
  12.7 19.7 %all-to-all-start = ((bf16[16,8,576]{2,1,0:T(8,128)(2,1)}), bf16[16,8,576]{2,1,0:T(8,128)(2,1)S(1)}, u32[]{:S(2)}, u32[]{:S(2)}) async-start(bf16[16,8,576]{2,1,0:T(8,128)(2,1)} %broadcast_in_dim.21), calls=%async_computation | async-start | bytes 327680 | tf_op jit(solution)/shard_map/prompt_gather/all_to_all | solution.py:383
  32.4 4.0 %copy-start.8 = (bf16[16,8,576]{2,1,0:T(8,128)(2,1)}, bf16[16,8,576]{2,1,0:T(8,128)(2,1)S(1)}, u32[]{:S(2)}) copy-start(bf16[16,8,576]{2,1,0:T(8,128)(2,1)S(1)} %all-to-all-done.rows_ref) | copy-start | bytes 442372
  32.4 27.7 %collective-permute-start.4 = (bf16[4,2,2,128,512]{4,3,2,1,0:T(8,128)(2,1)}, bf16[4,2,2,128,512]{4,3,2,1,0:T(8,128)(2,1)S(1)}, u32[]{:S(2)}, u32[]{:S(2)}) collective-permute-start(bf16[4,2,2,128,512]{4,3,2,1,0:T(8,128)(2,1)} %pad_maximum_fusion.refs_0_), channel_id=1, source_target_pairs={{0,4},{1,5},{2,6},{3,7},{4,8},{5,9},{6,10},{7,11},{8,12},{9,13},{1... | collective-permute-start | bytes 6291464 | tf_op jit(solution)/shard_map/weights_second_ring/ppermute | solution.py:44
  32.6 27.6 %collective-permute-start.5 = (bf16[4,2,2,128,512]{4,3,2,1,0:T(8,128)(2,1)}, bf16[4,2,2,128,512]{4,3,2,1,0:T(8,128)(2,1)}, u32[]{:S(2)}, u32[]{:S(2)}) collective-permute-start(bf16[4,2,2,128,512]{4,3,2,1,0:T(8,128)(2,1)} %pad_maximum_fusion.refs_0_), channel_id=1, source_target_pairs={{0,44},{1,45},{2,46},{3,47},{4,0},{5,1},{6,2},{7,3},{8,4},{9,5},{1... | collective-permute-start | bytes 6291464 | tf_op jit(solution)/shard_map/weights_second_ring/ppermute | solution.py:44
  35.1 46.5 %collective-permute-start.8 = (bf16[4,2,2,128,512]{4,3,2,1,0:T(8,128)(2,1)}, bf16[4,2,2,128,512]{4,3,2,1,0:T(8,128)(2,1)}, u32[]{:S(2)}, u32[]{:S(2)}) collective-permute-start(bf16[4,2,2,128,512]{4,3,2,1,0:T(8,128)(2,1)} %pad_maximum_fusion.refs_0_), channel_id=1, source_target_pairs={{0,16},{1,17},{2,18},{3,19},{4,20},{5,21},{6,22},{7,23},{8,24},{9,... | collective-permute-start | bytes 6291464 | tf_op jit(solution)/shard_map/weights_second_ring/ppermute | solution.py:44
  60.1 1.4 copy-start.5
  64.1 33.3 %collective-permute-start.6 = (bf16[2,2,2,128,512]{4,3,2,1,0:T(8,128)(2,1)}, bf16[2,2,2,128,512]{4,3,2,1,0:T(8,128)(2,1)}, u32[]{:S(2)}, u32[]{:S(2)}) collective-permute-start(bf16[2,2,2,128,512]{4,3,2,1,0:T(8,128)(2,1)} %get-tuple-element.31), channel_id=1, source_target_pairs={{0,4},{1,5},{2,6},{3,7},{4,8},{5,9},{6,10},{7,11},{8,12},{9,13},{1... | collective-permute-start | bytes 3145736 | tf_op jit(solution)/shard_map/weights_opposite/ppermute | solution.py:44
  64.6 34.6 %collective-permute-start.11 = (bf16[4,2,2,128,512]{4,3,2,1,0:T(8,128)(2,1)}, bf16[4,2,2,128,512]{4,3,2,1,0:T(8,128)(2,1)S(1)}, u32[]{:S(2)}, u32[]{:S(2)}) collective-permute-start(bf16[4,2,2,128,512]{4,3,2,1,0:T(8,128)(2,1)} %copy-done.5), channel_id=1, source_target_pairs={{0,16},{1,17},{2,18},{3,19},{4,20},{5,21},{6,22},{7,23},{8,24},{9,... | collective-permute-start | bytes 6291464 | tf_op jit(solution)/shard_map/weights_opposite/ppermute | solution.py:44
  71.6 27.6 %collective-permute-start.12 = (bf16[4,2,2,128,512]{4,3,2,1,0:T(8,128)(2,1)}, bf16[4,2,2,128,512]{4,3,2,1,0:T(8,128)(2,1)}, u32[]{:S(2)}, u32[]{:S(2)}) collective-permute-start(bf16[4,2,2,128,512]{4,3,2,1,0:T(8,128)(2,1)} %collective-permute-done.5.high_in.refs_3_), channel_id=1, source_target_pairs={{0,16},{1,17},{2,18},{3,19},{4,20},{5,21},{6,22},{7,23},{8,24},{9,... | collective-permute-start | bytes 6291464 | tf_op jit(solution)/shard_map/weights_opposite/ppermute | solution.py:44
  71.6 25.8 %collective-permute-start.7 = (bf16[2,2,2,128,512]{4,3,2,1,0:T(8,128)(2,1)}, bf16[2,2,2,128,512]{4,3,2,1,0:T(8,128)(2,1)}, u32[]{:S(2)}, u32[]{:S(2)}) collective-permute-start(bf16[2,2,2,128,512]{4,3,2,1,0:T(8,128)(2,1)} %get-tuple-element.32), channel_id=1, source_target_pairs={{0,44},{1,45},{2,46},{3,47},{4,0},{5,1},{6,2},{7,3},{8,4},{9,5},{1... | collective-permute-start | bytes 3145736 | tf_op jit(solution)/shard_map/weights_opposite/ppermute | solution.py:44
  73.1 4.4 %copy-start.7 = (bf16[128,64,128]{2,1,0:T(8,128)(2,1)S(1)}, bf16[128,64,128]{2,1,0:T(8,128)(2,1)}, u32[]{:S(2)}) copy-start(bf16[128,64,128]{2,1,0:T(8,128)(2,1)} %param.36) | copy-start | bytes 6291460
  77.5 3.9 %copy-start.11 = (s32[8]{0:T(128)S(1)}, s32[8]{0:T(128)}, u32[]{:S(2)}) copy-start(s32[8]{0:T(128)} %constant.69.clone) | copy-start | bytes 100
  77.5 3.9 %copy-start.12 = (s32[8]{0:T(128)S(1)}, s32[8]{0:T(128)}, u32[]{:S(2)}) copy-start(s32[8]{0:T(128)} %constant.70.clone) | copy-start | bytes 100
  77.5 3.9 %copy-start.13 = (s32[4]{0:T(128)S(1)}, s32[4]{0:T(128)}, u32[]{:S(2)}) copy-start(s32[4]{0:T(128)} %constant.67.clone) | copy-start | bytes 52
  77.5 4.0 %copy-start.10 = (s32[1,128]{1,0:T(1,128)S(1)}, s32[1,128]{1,0:T(1,128)}, u32[]{:S(2)}) copy-start(s32[1,128]{1,0:T(1,128)} %param.43) | copy-start | bytes 1540
  77.5 4.1 %copy-start = (bf16[128,4096]{1,0:T(8,128)(2,1)S(1)}, bf16[128,4096]{1,0:T(8,128)(2,1)}, u32[]{:S(2)}) copy-start(bf16[128,4096]{1,0:T(8,128)(2,1)} %refs_15_.4) | copy-start | bytes 3145732
  77.5 4.1 %copy-start.2 = (bf16[16,8,576]{2,1,0:T(8,128)(2,1)S(1)}, bf16[16,8,576]{2,1,0:T(8,128)(2,1)}, u32[]{:S(2)}) copy-start(bf16[16,8,576]{2,1,0:T(8,128)(2,1)} %all_to_all.20) | copy-start | bytes 442372
  77.5 4.1 %copy-start.3 = (s32[16,16]{1,0:T(8,128)S(1)}, s32[16,16]{1,0:T(8,128)}, u32[]{:S(2)}) copy-start(s32[16,16]{1,0:T(8,128)} %prompt_ref.3) | copy-start | bytes 3076
  77.6 4.1 %copy-start.4 = (s32[16]{0:T(128)S(1)}, s32[16]{0:T(128)}, u32[]{:S(2)}) copy-start(s32[16]{0:T(128)} %prompt_len_ref.5) | copy-start | bytes 196
  97.4 14.1 %collective-permute-start.10 = (bf16[2,2,2,128,512]{4,3,2,1,0:T(8,128)(2,1)}, bf16[2,2,2,128,512]{4,3,2,1,0:T(8,128)(2,1)S(1)}, u32[]{:S(2)}, u32[]{:S(2)}) collective-permute-start(bf16[2,2,2,128,512]{4,3,2,1,0:T(8,128)(2,1)} %collective-permute-done.7.refs_1_), channel_id=1, source_target_pairs={{0,16},{1,17},{2,18},{3,19},{4,20},{5,21},{6,22},{7,23},{8,24},{9,... | collective-permute-start | bytes 3145736 | tf_op jit(solution)/shard_map/ppermute | solution.py:44
  98.9 12.6 %collective-permute-start.9 = (bf16[2,2,2,128,512]{4,3,2,1,0:T(8,128)(2,1)}, bf16[2,2,2,128,512]{4,3,2,1,0:T(8,128)(2,1)S(1)}, u32[]{:S(2)}, u32[]{:S(2)}) collective-permute-start(bf16[2,2,2,128,512]{4,3,2,1,0:T(8,128)(2,1)} %collective-permute-done.6.refs_0_), channel_id=1, source_target_pairs={{0,16},{1,17},{2,18},{3,19},{4,20},{5,21},{6,22},{7,23},{8,24},{9,... | collective-permute-start | bytes 3145736 | tf_op jit(solution)/shard_map/ppermute | solution.py:44
  99.1 1.3 copy-start.6
  110.2 1.3 copy-start.1
  137.4 16.2 %all-to-all-start.3 = ((bf16[16,8,576]{2,1,0:T(8,128)(2,1)}), bf16[16,8,576]{2,1,0:T(8,128)(2,1)S(1)}, u32[]{:S(2)}, u32[]{:S(2)}) async-start(bf16[16,8,576]{2,1,0:T(8,128)(2,1)} %collect.1), calls=%async_computation.3 | async-start | bytes 327680 | tf_op jit(solution)/shard_map/prompt_return/all_to_all | solution.py:432

commit v2 on v1

--- a/solution.py
+++ b/solution.py
@@ -295,29 +295,6 @@
     )(*scalars, *operands)
 
 
-def halves_kernel(low_in, high_in, _, low, high):
-    low[...] = low_in[...]
-    high[...] = high_in[...]
-
-
-def halves(low, high, before):
-    n, *rest = low.shape
-    n //= 2
-
-    def block(begin):
-        return pl.BlockSpec((1, *rest), lambda i: (begin + i,) + (0,) * len(rest))
-
-    shape = jax.ShapeDtypeStruct((n, *rest), low.dtype)
-    return pl.pallas_call(
-        halves_kernel,
-        out_shape=(shape, shape),
-        grid=(n,),
-        in_specs=[block(0), block(n), pl.BlockSpec(memory_space=pl.ANY)],
-        out_specs=[block(0), block(0)],
-        name="halves",
-    )(low, high, before)
-
-
 def small_call(kernel, prompt_of, rows, dtype, scratch, name):
     block = pl.BlockSpec(rows.shape, lambda i, *_: (0, 0, 0))
     return pl.pallas_call(
@@ -383,10 +360,10 @@
         column = lax.all_to_all(copies, "dp", 0, 0, tiled=True)
 
     with jax.named_scope("weights_second_ring"):
-        near = jnp.stack([here, before, after, opposite])
-        near, column = lax.optimization_barrier((near, column))
-        middle = [second_ring(near, 1), second_ring(near, -1)]
-        near_peer = swap(near)
+        low, high = jnp.stack([here, before]), jnp.stack([after, opposite])
+        low, high, column = lax.optimization_barrier((low, high, column))
+        lead = [second_ring(low, 1), second_ring(high, -1)]
+        near_peer = [swap(low), swap(high)]
 
     with jax.named_scope("prompt_exchange"):
         prompt_rows = lax.all_to_all(select(prompt_of, column), "seq", 0, 0, tiled=True).reshape(prompts, WIDTH)
@@ -401,9 +378,10 @@
             dz = jnp.where(kind == 0, table[:, 1], table[:, 0])
             return (((z_lo + dz) & 3) * NX + ((x + dx) & 3)) * 2 + kind
 
-        first_pairs = jnp.concatenate([numbers(0, (0, order)), numbers(1, (0, order)), numbers(0, (-1, order), (1, order))])
-        peer_pairs = numbers(1, (-1, order), (1, order))
-        far_pairs = jnp.concatenate([numbers(side, (2, order[:2]), (2, order[2:])) for side in range(2)])
+        near_pairs = jnp.concatenate([numbers(side, (0, order)) for side in range(2)])
+        lead_pairs = jnp.concatenate([numbers(side, (-1, order[:2]), (1, order[2:])) for side in range(2)])
+        rest_blocks = (-1, order[2:]), (1, order[:2]), (2, order[:2]), (2, order[2:])
+        rest_pairs = [numbers(side, *rest_blocks) for side in range(2)]
 
     q = query_nope.reshape(tokens, heads // 2, 2, NOPE).transpose(1, 2, 0, 3)
     g = out_grad.reshape(tokens, heads // 2, 2, NOPE).transpose(1, 2, 0, 3)
@@ -416,16 +394,17 @@
         scalars = (pairs, prompt_of, prompt_len)
         return attention(sources, scalars, q, g, query_rope, prompt_rows, latent_rows, own_bias, state, last)
 
-    with jax.named_scope("weights_opposite"):
-        *middle, low, high = lax.optimization_barrier((*middle, *halves(*middle, prompt_rows)))
-        far = [second_ring(low, 1), second_ring(high, -1)]
-        middle_peer = [swap(w) for w in middle]
-    state = work([near, near_peer, *middle], first_pairs, None)
-    *far, turn = lax.optimization_barrier((*far, state[1]))
+    with jax.named_scope("weights_rest"):
+        low, high, *lead, prompt_rows = lax.optimization_barrier((low, high, *lead, prompt_rows))
+        rest = [second_ring(high, 1), second_ring(low, -1), second_ring(lead[0], 1), second_ring(lead[1], -1)]
+        lead_peer = [swap(w) for w in lead]
+    state = work([low, high, *near_peer], near_pairs, None)
+    state = work([*lead, *lead_peer], lead_pairs, state)
+    *rest, turn = lax.optimization_barrier((*rest, state[1]))
     state = (state[0], turn, *state[2:])
-    far_peer = [swap(w) for w in far]
-    state = work(middle_peer, peer_pairs, state)
-    prompt_part, grad_latent, grad_nope, grad_rope = work([*far, *far_peer], far_pairs, state, last=True)
+    rest_peer = [swap(w) for w in rest]
+    state = work(rest, rest_pairs[0], state)
+    prompt_part, grad_latent, grad_nope, grad_rope = work(rest_peer, rest_pairs[1], state, last=True)
 
     with jax.named_scope("prompt_return"):
         parts = lax.all_to_all(prompt_part.reshape(members, rows, WIDTH), "seq", 0, 0, tiled=True)

time: 155 us -> 139 us (0.90)
  blocking collectives: 35.8 us -> 14.4 us
  waiting for transfers between devices: 14.2 us -> 21.5 us
  starting transfers between devices: 39.9 us -> 44.1 us
  Pallas kernels: 41.9 us -> 38.2 us
  local copies, waits for them, and re-layouts: 18 us -> 15.7 us
    all_to_all x1 -> x0, blocking collectives: 21.3 us -> none  [local(): lax.all_to_all(select(prompt_of, column), 'seq', 0, 0, tiled=True)]
    all_to_all x0 -> x1, waiting for transfers between devices: none -> 7.67 us  [local(): lax.all_to_all(select(prompt_of, column), 'seq', 0, 0, tiled=True)]
    all_to_all x0 -> x1, starting transfers between devices: none -> 4.28 us  [local(): lax.all_to_all(select(prompt_of, column), 'seq', 0, 0, tiled=True)]
    pallas_call x1 -> x0, Pallas kernels: 2.57 us -> none  [halves(): pl.pallas_call(halves_kernel, out_shape=(shape, shape), grid=(n,), in_spe...]
    unnamed x33 -> x31, local copies, waits for them, and re-layouts: 17.3 us -> 15 us
    pallas_call x3 -> x4, Pallas kernels: 34.4 us -> 33.3 us  [attention(): pl.pallas_call(functools.partial(attention_kernel, counts, first, last),...]
    ppermute x13 -> x18, starting transfers between devices: 24.8 us -> 23.8 us  [permute(): return lax.ppermute(array, AXES, pairs)]
  transfers between devices with their start and end apart: 15 -> 21, of which waited for: 2 -> 5; matrix products, arithmetic and copies ran while one was open for 10% -> 11% of each run, Pallas kernels for 20% -> 20%
where the time goes in v2:
time: 139 us; the launch traced here: 138 us
  starting transfers between devices  44.1 us (32%)
  Pallas kernels  38.2 us (27%)
  waiting for transfers between devices  21.5 us (15%)
  local copies, waits for them, and re-layouts  15.7 us (11%)
  blocking collectives  14.4 us (10%)
  other arithmetic  3.27 us (2%)
    pallas_call x4, Pallas kernels, attention(): pl.pallas_call(functools.partial(attention_kernel, counts, first, last),...  33.3 us
    ppermute x18, starting transfers between devices, permute(): return lax.ppermute(array, AXES, pairs)  23.8 us
    unnamed x31, local copies, waits for them, and re-layouts  15 us
    all_to_all x1, blocking collectives, local(): lax.all_to_all(prompt_part.reshape(members, rows, WIDTH), 'seq', 0, 0, ti...  14.4 us
    all_to_all x1, starting transfers between devices, local(): column = lax.all_to_all(copies, 'dp', 0, 0, tiled=True)  10.6 us
    all_to_all x1, waiting for transfers between devices, local(): column = lax.all_to_all(copies, 'dp', 0, 0, tiled=True)  8.03 us
    all_to_all x1, waiting for transfers between devices, local(): lax.all_to_all(select(prompt_of, column), 'seq', 0, 0, tiled=True)  7.67 us
    all_to_all x1, starting transfers between devices, local(): sums = lax.all_to_all(collect(prompt_of, parts), 'dp', 0, 0, tiled=True)  5.44 us
  transfers between devices with their start and end apart: 21, of which 5 were waited for; matrix products, arithmetic and copies ran while one was open for 11% of the time, Pallas kernels for 20%

profile of v2, /device:TPU:1, one launch (start us, length us, event | category | flops | bytes accessed | tf_op | source)
XLA Modules:
  0.0 138.2 jit_solution(1021926240590481933)
XLA Ops:
  0.7 1.1 fusion
  1.7 2.5 %collective-permute-start = (bf16[2,2,128,512]{3,2,1,0:T(8,128)(2,1)S(1)}, bf16[2,2,128,512]{3,2,1,0:T(8,128)(2,1)S(1)}, u32[]{:S(2)}, u32[]{:S(2)}) collective-permute-start(bf16[2,2,128,512]{3,2,1,0:T(8,128)(2,1)S(1)} %bitcast.65), channel_id=1, source_target_pairs={{0,1},{1,2},{2,3},{3,0},{4,5},{5,6},{6,7},{7,4},{8,9},{9,10},{10,1... | collective-permute-start | bytes 1572872 | tf_op jit(solution)/shard_map/weights_first_ring/ppermute | solution.py:44
  4.3 3.1 %collective-permute-start.2 = (bf16[2,128,512]{2,1,0:T(8,128)(2,1)S(1)}, bf16[2,128,512]{2,1,0:T(8,128)(2,1)S(1)}, u32[]{:S(2)}, u32[]{:S(2)}) collective-permute-start(bf16[2,128,512]{2,1,0:T(8,128)(2,1)S(1)} %get-tuple-element.66), channel_id=1, source_target_pairs={{0,2},{1,3},{2,0},{3,1},{4,6},{5,7},{6,4},{7,5},{8,10},{9,11},{10,... | collective-permute-start | bytes 786440 | tf_op jit(solution)/shard_map/weights_first_ring/ppermute | solution.py:44
  7.4 2.2 %collective-permute-start.3 = (bf16[2,128,512]{2,1,0:T(8,128)(2,1)S(1)}, bf16[2,128,512]{2,1,0:T(8,128)(2,1)S(1)}, u32[]{:S(2)}, u32[]{:S(2)}) collective-permute-start(bf16[2,128,512]{2,1,0:T(8,128)(2,1)S(1)} %get-tuple-element.67), channel_id=1, source_target_pairs={{0,2},{1,3},{2,0},{3,1},{4,6},{5,7},{6,4},{7,5},{8,10},{9,11},{10,... | collective-permute-start | bytes 786440 | tf_op jit(solution)/shard_map/weights_first_ring/ppermute | solution.py:44
  9.6 1.1 collective-permute-start.1
  10.7 0.7 broadcast_in_dim.21
  11.4 10.6 %all-to-all-start = ((bf16[16,8,576]{2,1,0:T(8,128)(2,1)}), bf16[16,8,576]{2,1,0:T(8,128)(2,1)S(1)}, u32[]{:S(2)}, u32[]{:S(2)}) async-start(bf16[16,8,576]{2,1,0:T(8,128)(2,1)} %broadcast_in_dim.21), calls=%async_computation | async-start | bytes 327680 | tf_op jit(solution)/shard_map/prompt_gather/all_to_all | solution.py:360
  22.0 0.0 collective-permute-done.2
  22.0 0.0 collective-permute-done.3
  22.0 0.1 maximum_bitcast_fusion
  22.1 0.0 collective-permute-done
  22.1 0.1 pad_maximum_fusion.refs_0_
  22.2 0.3 collective-permute-done.1
  22.5 0.8 copy-done.6
  23.3 1.1 pad_maximum_fusion.1.refs_1_
  24.4 8.0 %all-to-all-done.rows_ref = bf16[16,8,576]{2,1,0:T(8,128)(2,1)S(1)} async-done(((bf16[16,8,576]{2,1,0:T(8,128)(2,1)}), bf16[16,8,576]{2,1,0:T(8,128)(2,1)S(1)}, u32[]{:S(2)}, u32[]{:S(2)}) %all-to-all-start) | async-done | bytes 147488 | tf_op jit(solution)/shard_map/prompt_gather/all_to_all | solution.py:360
  32.4 2.7 %collective-permute-start.5 = (bf16[2,2,2,128,512]{4,3,2,1,0:T(8,128)(2,1)S(1)}, bf16[2,2,2,128,512]{4,3,2,1,0:T(8,128)(2,1)}, u32[]{:S(2)}, u32[]{:S(2)}) collective-permute-start(bf16[2,2,2,128,512]{4,3,2,1,0:T(8,128)(2,1)S(1)} %pad_maximum_fusion.1.refs_1_), channel_id=1, source_target_pairs={{0,44},{1,45},{2,46},{3,47},{4,0},{5,1},{6,2},{7,3},{8,4},{9,5},{1... | collective-permute-start | bytes 3145736 | tf_op jit(solution)/shard_map/weights_second_ring/ppermute | solution.py:44
  35.1 2.4 %select.9 = bf16[16,8,576]{2,1,0:T(8,128)(2,1)} custom-call(s32[16,16]{1,0:T(8,128)} %prompt_ref.3, bf16[16,8,576]{2,1,0:T(8,128)(2,1)} %copy-done.5), custom_call_target="tpu_custom_call" | custom-call | tf_op jit(solution)/shard_map/prompt_exchange/select/pallas_call | solution.py:300
  37.5 4.3 %all-to-all-start.1 = ((bf16[16,8,576]{2,1,0:T(8,128)(2,1)}), bf16[16,8,576]{2,1,0:T(8,128)(2,1)S(1)}, u32[]{:S(2)}, u32[]{:S(2)}) async-start(bf16[16,8,576]{2,1,0:T(8,128)(2,1)} %select.9), calls=%async_computation.1 | async-start | bytes 327680 | tf_op jit(solution)/shard_map/prompt_exchange/all_to_all | solution.py:369
  41.8 1.7 %collective-permute-start.12 = (bf16[2,2,2,128,512]{4,3,2,1,0:T(8,128)(2,1)S(1)}, bf16[2,2,2,128,512]{4,3,2,1,0:T(8,128)(2,1)}, u32[]{:S(2)}, u32[]{:S(2)}) collective-permute-start(bf16[2,2,2,128,512]{4,3,2,1,0:T(8,128)(2,1)S(1)} %pad_maximum_fusion.refs_0_), channel_id=1, source_target_pairs={{0,16},{1,17},{2,18},{3,19},{4,20},{5,21},{6,22},{7,23},{8,24},{9,... | collective-permute-start | bytes 3145736 | tf_op jit(solution)/shard_map/weights_second_ring/ppermute | solution.py:44
  43.4 0.1 collective-permute-start.13
  43.5 7.7 %all-to-all-done.1 = bf16[16,8,576]{2,1,0:T(8,128)(2,1)S(1)} async-done(((bf16[16,8,576]{2,1,0:T(8,128)(2,1)}), bf16[16,8,576]{2,1,0:T(8,128)(2,1)S(1)}, u32[]{:S(2)}, u32[]{:S(2)}) %all-to-all-start.1) | async-done | bytes 147488 | tf_op jit(solution)/shard_map/prompt_exchange/all_to_all | solution.py:369
  51.2 0.0 collective-permute-done.4.refs_0_
  51.2 0.0 collective-permute-done.5.refs_1_
  51.2 4.1 %collective-permute-start.10 = (bf16[2,2,2,128,512]{4,3,2,1,0:T(8,128)(2,1)}, bf16[2,2,2,128,512]{4,3,2,1,0:T(8,128)(2,1)S(1)}, u32[]{:S(2)}, u32[]{:S(2)}) collective-permute-start(bf16[2,2,2,128,512]{4,3,2,1,0:T(8,128)(2,1)} %collective-permute-done.4.refs_0_), channel_id=1, source_target_pairs={{0,16},{1,17},{2,18},{3,19},{4,20},{5,21},{6,22},{7,23},{8,24},{9,... | collective-permute-start | bytes 3145736 | tf_op jit(solution)/shard_map/weights_rest/ppermute | solution.py:44
  55.3 0.1 collective-permute-start.11
  55.4 0.2 collective-permute-start.8
  55.6 0.9 collective-permute-start.6
  56.4 0.0 collective-permute-done.13.refs_3_
  56.4 1.8 %collective-permute-start.7 = (bf16[2,2,2,128,512]{4,3,2,1,0:T(8,128)(2,1)S(1)}, bf16[2,2,2,128,512]{4,3,2,1,0:T(8,128)(2,1)}, u32[]{:S(2)}, u32[]{:S(2)}) collective-permute-start(bf16[2,2,2,128,512]{4,3,2,1,0:T(8,128)(2,1)S(1)} %pad_maximum_fusion.refs_0_), channel_id=1, source_target_pairs={{0,44},{1,45},{2,46},{3,47},{4,0},{5,1},{6,2},{7,3},{8,4},{9,5},{1... | collective-permute-start | bytes 3145736 | tf_op jit(solution)/shard_map/weights_rest/ppermute | solution.py:44
  58.3 0.1 collective-permute-done.10.refs_2_
  58.3 1.0 copy-done
  59.3 1.5 %collective-permute-start.9 = (bf16[2,2,2,128,512]{4,3,2,1,0:T(8,128)(2,1)}, bf16[2,2,2,128,512]{4,3,2,1,0:T(8,128)(2,1)}, u32[]{:S(2)}, u32[]{:S(2)}) collective-permute-start(bf16[2,2,2,128,512]{4,3,2,1,0:T(8,128)(2,1)} %collective-permute-done.5.refs_1_), channel_id=1, source_target_pairs={{0,44},{1,45},{2,46},{3,47},{4,0},{5,1},{6,2},{7,3},{8,4},{9,5},{1... | collective-permute-start | bytes 3145736 | tf_op jit(solution)/shard_map/weights_rest/ppermute | solution.py:44
  60.8 4.4 %copy.44 = bf16[128,64,128]{2,0,1:T(8,128)(2,1)} copy(bf16[128,64,128]{2,1,0:T(8,128)(2,1)} %param.34) | data formatting | bytes 4194304 | tf_op args[0]
  65.3 0.0 copy-start.2
  65.3 0.0 copy-start.3
  65.3 2.7 %copy.45 = bf16[128,64,128]{2,0,1:T(8,128)(2,1)} copy(bf16[128,64,128]{2,1,0:T(8,128)(2,1)S(1)} %copy-done.4) | data formatting | bytes 4194304 | tf_op args[2]
  68.0 1.1 copy.47.refs_17_
  69.1 0.1 pad_add_fusion.1.pair_ref
  69.2 0.1 pad_add_fusion.pair_ref
  69.3 0.1 fusion.2.refs_18_
  69.4 7.6 %attention.4 = (f32[256,512]{1,0:T(8,128)S(1)}, f32[256,128]{1,0:T(8,128)S(1)}, bf16[32,2,128,128]{3,2,1,0:T(8,128)(2,1)}, bf16[128,4096]{1,0:T(8,128)(2,1)}) custom-call(s32[8]{0:T(128)S(1)} %pad_add_fusion.1.pair_ref, s32[16,16]{1,0:T(8,128)S(1)} %copy-done.2, s32[16]{0:T(128)S(1)} %copy-done.3, bf16[2,2,2,128,512]{4,3,2,1,0:T(8,128)(2,1)S(1)} %pad_maximum_fusion.refs_0_, ...), custom_call_target="tpu_custom_call" | custom-call | tf_op jit(solution)/shard_map/attention/pallas_call | solution.py:268
  77.0 0.0 collective-permute-done.11.refs_3_
  77.0 0.0 copy-start.9
  77.1 0.0 copy-start.10
  77.1 9.0 %attention.5 = (f32[256,512]{1,0:T(8,128)S(1)}, f32[256,128]{1,0:T(8,128)S(1)}, bf16[32,2,128,128]{3,2,1,0:T(8,128)(2,1)}, bf16[128,4096]{1,0:T(8,128)(2,1)}) custom-call(s32[8]{0:T(128)S(1)} %pad_add_fusion.pair_ref, s32[16,16]{1,0:T(8,128)S(1)} %copy-done.2, s32[16]{0:T(128)S(1)} %copy-done.3, ...), custom_call_target="tpu_custom_call", output_to_operand_aliasing={{2}: (24, {}), {3}: (25, {})} | custom-call | tf_op jit(solution)/shard_map/attention/pallas_call | solution.py:268
  86.1 0.0 collective-permute-done.7.refs_1_
  86.1 0.0 collective-permute-done.8.refs_2_
  86.1 1.3 collective-permute-start.14
  87.4 0.1 collective-permute-start.15
  87.5 0.4 collective-permute-start.16
  87.9 0.1 collective-permute-start.17
  88.0 9.0 %attention.6 = (f32[256,512]{1,0:T(8,128)S(1)}, f32[256,128]{1,0:T(8,128)S(1)}, bf16[32,2,128,128]{3,2,1,0:T(8,128)(2,1)}, bf16[128,4096]{1,0:T(8,128)(2,1)}) custom-call(s32[8]{0:T(128)S(1)} %get-tuple-element.68.pair_ref, s32[16,16]{1,0:T(8,128)S(1)} %copy-done.2, s32[16]{0:T(128)S(1)} %copy-done.3, ...), custom_call_target="tpu_custom_call", output_to_operand_aliasing={{2}: (24, {}), {3}: (25, {})} | custom-call | tf_op jit(solution)/shard_map/attention/pallas_call | solution.py:268
  97.0 0.0 collective-permute-done.14.refs_0_
  97.0 0.0 collective-permute-done.15.refs_1_
  97.0 0.0 collective-permute-done.17.refs_3_
  97.0 7.8 %attention.7 = (f32[128,576]{1,0:T(8,128)S(1)}, bf16[128,576]{1,0:T(8,128)(2,1)S(1)}, bf16[32,2,128,128]{3,2,1,0:T(8,128)(2,1)}, bf16[128,4096]{1,0:T(8,128)(2,1)}) custom-call(s32[8]{0:T(128)S(1)} %get-tuple-element.69.pair_ref, s32[16,16]{1,0:T(8,128)S(1)} %copy-done.2, s32[16]{0:T(128)S(1)} %copy-done.3, ...), custom_call_target="tpu_custom_call", output_to_operand_aliasing={{2}: (24, {}), {3}: (25, {})} | custom-call | tf_op jit(solution)/shard_map/attention/pallas_call | solution.py:268
  104.8 14.4 %all_to_all.20.parts_ref = f32[16,8,576]{2,1,0:T(8,128)} all-to-all(f32[16,8,576]{2,1,0:T(8,128)S(1)} %bitcast.31), channel_id=1, replica_groups=mesh['dp'=16,'seq'=16] {'seq'}, dimensions={0} | all-to-all | bytes 589824 | tf_op jit(solution)/shard_map/prompt_return/all_to_all | solution.py:410
  119.2 2.5 %collect.1 = bf16[16,8,576]{2,1,0:T(8,128)(2,1)} custom-call(s32[16,16]{1,0:T(8,128)} %prompt_ref.3, f32[16,8,576]{2,1,0:T(8,128)} %all_to_all.20.parts_ref), custom_call_target="tpu_custom_call" | custom-call | tf_op jit(solution)/shard_map/prompt_return/collect/pallas_call | solution.py:300
  121.7 5.4 %all-to-all-start.3 = ((bf16[16,8,576]{2,1,0:T(8,128)(2,1)}), bf16[16,8,576]{2,1,0:T(8,128)(2,1)S(1)}, u32[]{:S(2)}, u32[]{:S(2)}) async-start(bf16[16,8,576]{2,1,0:T(8,128)(2,1)} %collect.1), calls=%async_computation.3 | async-start | bytes 327680 | tf_op jit(solution)/shard_map/prompt_return/all_to_all | solution.py:411
  127.1 4.3 %copy.50 = bf16[128,64,128]{2,1,0:T(8,128)(2,1)} copy(bf16[128,64,128]{2,0,1:T(8,128)(2,1)} %bitcast.64) | data formatting | bytes 4194304
  131.4 0.8 copy.51
  132.2 5.4 %all-to-all-done.3 = bf16[16,8,576]{2,1,0:T(8,128)(2,1)S(1)} async-done(((bf16[16,8,576]{2,1,0:T(8,128)(2,1)}), bf16[16,8,576]{2,1,0:T(8,128)(2,1)S(1)}, u32[]{:S(2)}, u32[]{:S(2)}) %all-to-all-start.3) | async-done | bytes 147488 | tf_op jit(solution)/shard_map/prompt_return/all_to_all | solution.py:411
  137.6 0.6 convert_reduce_fusion
  (28 shorter events, 0.1 us)
Async XLA Ops:
  0.6 10.1 %copy-start.7 = (bf16[1,8,576]{2,1,0:T(8,128)(2,1)S(1)}, bf16[1,8,576]{2,1,0:T(8,128)(2,1)}, u32[]{:S(2)}) copy-start(bf16[1,8,576]{2,1,0:T(8,128)(2,1)} %param.38) | copy-start | bytes 27652
  1.7 20.3 %collective-permute-start = (bf16[2,2,128,512]{3,2,1,0:T(8,128)(2,1)S(1)}, bf16[2,2,128,512]{3,2,1,0:T(8,128)(2,1)S(1)}, u32[]{:S(2)}, u32[]{:S(2)}) collective-permute-start(bf16[2,2,128,512]{3,2,1,0:T(8,128)(2,1)S(1)} %bitcast.65), channel_id=1, source_target_pairs={{0,1},{1,2},{2,3},{3,0},{4,5},{5,6},{6,7},{7,4},{8,9},{9,10},{10,1... | collective-permute-start | bytes 1572872 | tf_op jit(solution)/shard_map/weights_first_ring/ppermute | solution.py:44
  4.3 17.7 %collective-permute-start.2 = (bf16[2,128,512]{2,1,0:T(8,128)(2,1)S(1)}, bf16[2,128,512]{2,1,0:T(8,128)(2,1)S(1)}, u32[]{:S(2)}, u32[]{:S(2)}) collective-permute-start(bf16[2,128,512]{2,1,0:T(8,128)(2,1)S(1)} %get-tuple-element.66), channel_id=1, source_target_pairs={{0,2},{1,3},{2,0},{3,1},{4,6},{5,7},{6,4},{7,5},{8,10},{9,11},{10,... | collective-permute-start | bytes 786440 | tf_op jit(solution)/shard_map/weights_first_ring/ppermute | solution.py:44
  7.4 14.6 %collective-permute-start.3 = (bf16[2,128,512]{2,1,0:T(8,128)(2,1)S(1)}, bf16[2,128,512]{2,1,0:T(8,128)(2,1)S(1)}, u32[]{:S(2)}, u32[]{:S(2)}) collective-permute-start(bf16[2,128,512]{2,1,0:T(8,128)(2,1)S(1)} %get-tuple-element.67), channel_id=1, source_target_pairs={{0,2},{1,3},{2,0},{3,1},{4,6},{5,7},{6,4},{7,5},{8,10},{9,11},{10,... | collective-permute-start | bytes 786440 | tf_op jit(solution)/shard_map/weights_first_ring/ppermute | solution.py:44
  9.6 12.9 %collective-permute-start.1 = (bf16[2,2,128,512]{3,2,1,0:T(8,128)(2,1)S(1)}, bf16[2,2,128,512]{3,2,1,0:T(8,128)(2,1)S(1)}, u32[]{:S(2)}, u32[]{:S(2)}) collective-permute-start(bf16[2,2,128,512]{3,2,1,0:T(8,128)(2,1)S(1)} %bitcast.66), channel_id=1, source_target_pairs={{0,3},{1,0},{2,1},{3,2},{4,7},{5,4},{6,5},{7,6},{8,11},{9,8},{10,9... | collective-permute-start | bytes 1572872 | tf_op jit(solution)/shard_map/weights_first_ring/ppermute | solution.py:44
  11.4 21.0 %all-to-all-start = ((bf16[16,8,576]{2,1,0:T(8,128)(2,1)}), bf16[16,8,576]{2,1,0:T(8,128)(2,1)S(1)}, u32[]{:S(2)}, u32[]{:S(2)}) async-start(bf16[16,8,576]{2,1,0:T(8,128)(2,1)} %broadcast_in_dim.21), calls=%async_computation | async-start | bytes 327680 | tf_op jit(solution)/shard_map/prompt_gather/all_to_all | solution.py:360
  22.5 0.8 copy-start.6
  32.4 2.7 %copy-start.5 = (bf16[16,8,576]{2,1,0:T(8,128)(2,1)}, bf16[16,8,576]{2,1,0:T(8,128)(2,1)S(1)}, u32[]{:S(2)}) copy-start(bf16[16,8,576]{2,1,0:T(8,128)(2,1)S(1)} %all-to-all-done.rows_ref) | copy-start | bytes 442372
  32.4 18.8 %collective-permute-start.4 = (bf16[2,2,2,128,512]{4,3,2,1,0:T(8,128)(2,1)S(1)}, bf16[2,2,2,128,512]{4,3,2,1,0:T(8,128)(2,1)}, u32[]{:S(2)}, u32[]{:S(2)}) collective-permute-start(bf16[2,2,2,128,512]{4,3,2,1,0:T(8,128)(2,1)S(1)} %pad_maximum_fusion.refs_0_), channel_id=1, source_target_pairs={{0,4},{1,5},{2,6},{3,7},{4,8},{5,9},{6,10},{7,11},{8,12},{9,13},{1... | collective-permute-start | bytes 3145736 | tf_op jit(solution)/shard_map/weights_second_ring/ppermute | solution.py:44
  32.4 18.8 %collective-permute-start.5 = (bf16[2,2,2,128,512]{4,3,2,1,0:T(8,128)(2,1)S(1)}, bf16[2,2,2,128,512]{4,3,2,1,0:T(8,128)(2,1)}, u32[]{:S(2)}, u32[]{:S(2)}) collective-permute-start(bf16[2,2,2,128,512]{4,3,2,1,0:T(8,128)(2,1)S(1)} %pad_maximum_fusion.1.refs_1_), channel_id=1, source_target_pairs={{0,44},{1,45},{2,46},{3,47},{4,0},{5,1},{6,2},{7,3},{8,4},{9,5},{1... | collective-permute-start | bytes 3145736 | tf_op jit(solution)/shard_map/weights_second_ring/ppermute | solution.py:44
  37.5 13.7 %all-to-all-start.1 = ((bf16[16,8,576]{2,1,0:T(8,128)(2,1)}), bf16[16,8,576]{2,1,0:T(8,128)(2,1)S(1)}, u32[]{:S(2)}, u32[]{:S(2)}) async-start(bf16[16,8,576]{2,1,0:T(8,128)(2,1)} %select.9), calls=%async_computation.1 | async-start | bytes 327680 | tf_op jit(solution)/shard_map/prompt_exchange/all_to_all | solution.py:369
  41.8 13.8 %collective-permute-start.12 = (bf16[2,2,2,128,512]{4,3,2,1,0:T(8,128)(2,1)S(1)}, bf16[2,2,2,128,512]{4,3,2,1,0:T(8,128)(2,1)}, u32[]{:S(2)}, u32[]{:S(2)}) collective-permute-start(bf16[2,2,2,128,512]{4,3,2,1,0:T(8,128)(2,1)S(1)} %pad_maximum_fusion.refs_0_), channel_id=1, source_target_pairs={{0,16},{1,17},{2,18},{3,19},{4,20},{5,21},{6,22},{7,23},{8,24},{9,... | collective-permute-start | bytes 3145736 | tf_op jit(solution)/shard_map/weights_second_ring/ppermute | solution.py:44
  43.4 13.0 %collective-permute-start.13 = (bf16[2,2,2,128,512]{4,3,2,1,0:T(8,128)(2,1)S(1)}, bf16[2,2,2,128,512]{4,3,2,1,0:T(8,128)(2,1)}, u32[]{:S(2)}, u32[]{:S(2)}) collective-permute-start(bf16[2,2,2,128,512]{4,3,2,1,0:T(8,128)(2,1)S(1)} %pad_maximum_fusion.1.refs_1_), channel_id=1, source_target_pairs={{0,16},{1,17},{2,18},{3,19},{4,20},{5,21},{6,22},{7,23},{8,24},{9,... | collective-permute-start | bytes 3145736 | tf_op jit(solution)/shard_map/weights_second_ring/ppermute | solution.py:44
  51.2 7.1 %collective-permute-start.10 = (bf16[2,2,2,128,512]{4,3,2,1,0:T(8,128)(2,1)}, bf16[2,2,2,128,512]{4,3,2,1,0:T(8,128)(2,1)S(1)}, u32[]{:S(2)}, u32[]{:S(2)}) collective-permute-start(bf16[2,2,2,128,512]{4,3,2,1,0:T(8,128)(2,1)} %collective-permute-done.4.refs_0_), channel_id=1, source_target_pairs={{0,16},{1,17},{2,18},{3,19},{4,20},{5,21},{6,22},{7,23},{8,24},{9,... | collective-permute-start | bytes 3145736 | tf_op jit(solution)/shard_map/weights_rest/ppermute | solution.py:44
  55.3 21.7 %collective-permute-start.11 = (bf16[2,2,2,128,512]{4,3,2,1,0:T(8,128)(2,1)}, bf16[2,2,2,128,512]{4,3,2,1,0:T(8,128)(2,1)}, u32[]{:S(2)}, u32[]{:S(2)}) collective-permute-start(bf16[2,2,2,128,512]{4,3,2,1,0:T(8,128)(2,1)} %collective-permute-done.5.refs_1_), channel_id=1, source_target_pairs={{0,16},{1,17},{2,18},{3,19},{4,20},{5,21},{6,22},{7,23},{8,24},{9,... | collective-permute-start | bytes 3145736 | tf_op jit(solution)/shard_map/weights_rest/ppermute | solution.py:44
  55.4 30.7 %collective-permute-start.8 = (bf16[2,2,2,128,512]{4,3,2,1,0:T(8,128)(2,1)}, bf16[2,2,2,128,512]{4,3,2,1,0:T(8,128)(2,1)S(1)}, u32[]{:S(2)}, u32[]{:S(2)}) collective-permute-start(bf16[2,2,2,128,512]{4,3,2,1,0:T(8,128)(2,1)} %collective-permute-done.4.refs_0_), channel_id=1, source_target_pairs={{0,4},{1,5},{2,6},{3,7},{4,8},{5,9},{6,10},{7,11},{8,12},{9,13},{1... | collective-permute-start | bytes 3145736 | tf_op jit(solution)/shard_map/weights_rest/ppermute | solution.py:44
  55.6 30.5 %collective-permute-start.6 = (bf16[2,2,2,128,512]{4,3,2,1,0:T(8,128)(2,1)S(1)}, bf16[2,2,2,128,512]{4,3,2,1,0:T(8,128)(2,1)}, u32[]{:S(2)}, u32[]{:S(2)}) collective-permute-start(bf16[2,2,2,128,512]{4,3,2,1,0:T(8,128)(2,1)S(1)} %pad_maximum_fusion.1.refs_1_), channel_id=1, source_target_pairs={{0,4},{1,5},{2,6},{3,7},{4,8},{5,9},{6,10},{7,11},{8,12},{9,13},{1... | collective-permute-start | bytes 3145736 | tf_op jit(solution)/shard_map/weights_rest/ppermute | solution.py:44
  56.4 29.6 %collective-permute-start.7 = (bf16[2,2,2,128,512]{4,3,2,1,0:T(8,128)(2,1)S(1)}, bf16[2,2,2,128,512]{4,3,2,1,0:T(8,128)(2,1)}, u32[]{:S(2)}, u32[]{:S(2)}) collective-permute-start(bf16[2,2,2,128,512]{4,3,2,1,0:T(8,128)(2,1)S(1)} %pad_maximum_fusion.refs_0_), channel_id=1, source_target_pairs={{0,44},{1,45},{2,46},{3,47},{4,0},{5,1},{6,2},{7,3},{8,4},{9,5},{1... | collective-permute-start | bytes 3145736 | tf_op jit(solution)/shard_map/weights_rest/ppermute | solution.py:44
  58.3 1.0 copy-start
  59.3 26.8 %collective-permute-start.9 = (bf16[2,2,2,128,512]{4,3,2,1,0:T(8,128)(2,1)}, bf16[2,2,2,128,512]{4,3,2,1,0:T(8,128)(2,1)}, u32[]{:S(2)}, u32[]{:S(2)}) collective-permute-start(bf16[2,2,2,128,512]{4,3,2,1,0:T(8,128)(2,1)} %collective-permute-done.5.refs_1_), channel_id=1, source_target_pairs={{0,44},{1,45},{2,46},{3,47},{4,0},{5,1},{6,2},{7,3},{8,4},{9,5},{1... | collective-permute-start | bytes 3145736 | tf_op jit(solution)/shard_map/weights_rest/ppermute | solution.py:44
  60.8 4.4 %copy-start.4 = (bf16[128,64,128]{2,1,0:T(8,128)(2,1)S(1)}, bf16[128,64,128]{2,1,0:T(8,128)(2,1)}, u32[]{:S(2)}) copy-start(bf16[128,64,128]{2,1,0:T(8,128)(2,1)} %param.36) | copy-start | bytes 6291460
  65.2 3.8 %copy-start.11 = (s32[4]{0:T(128)S(1)}, s32[4]{0:T(128)}, u32[]{:S(2)}) copy-start(s32[4]{0:T(128)} %constant.67.clone) | copy-start | bytes 52
  65.2 3.8 %copy-start.12 = (s32[4]{0:T(128)S(1)}, s32[4]{0:T(128)}, u32[]{:S(2)}) copy-start(s32[4]{0:T(128)} %constant.69.clone) | copy-start | bytes 52
  65.2 4.0 %copy-start.8 = (s32[1,128]{1,0:T(1,128)S(1)}, s32[1,128]{1,0:T(1,128)}, u32[]{:S(2)}) copy-start(s32[1,128]{1,0:T(1,128)} %param.43) | copy-start | bytes 1540
  65.3 4.1 %copy-start.2 = (s32[16,16]{1,0:T(8,128)S(1)}, s32[16,16]{1,0:T(8,128)}, u32[]{:S(2)}) copy-start(s32[16,16]{1,0:T(8,128)} %prompt_ref.3) | copy-start | bytes 3076
  65.3 4.1 %copy-start.3 = (s32[16]{0:T(128)S(1)}, s32[16]{0:T(128)}, u32[]{:S(2)}) copy-start(s32[16]{0:T(128)} %prompt_len_ref.7) | copy-start | bytes 196
  69.4 7.7 %copy-start.1 = (bf16[2,2,2,128,512]{4,3,2,1,0:T(8,128)(2,1)S(1)}, bf16[2,2,2,128,512]{4,3,2,1,0:T(8,128)(2,1)}, u32[]{:S(2)}) copy-start(bf16[2,2,2,128,512]{4,3,2,1,0:T(8,128)(2,1)} %copy-done) | copy-start | bytes 3145732
  77.0 10.9 %copy-start.9 = (s32[8]{0:T(128)S(1)}, s32[8]{0:T(128)}, u32[]{:S(2)}) copy-start(s32[8]{0:T(128)} %constant.70.clone) | copy-start | bytes 100
  77.1 10.9 %copy-start.10 = (s32[8]{0:T(128)S(1)}, s32[8]{0:T(128)}, u32[]{:S(2)}) copy-start(s32[8]{0:T(128)} %constant.71.clone) | copy-start | bytes 100
  86.1 10.9 %collective-permute-start.14 = (bf16[2,2,2,128,512]{4,3,2,1,0:T(8,128)(2,1)}, bf16[2,2,2,128,512]{4,3,2,1,0:T(8,128)(2,1)S(1)}, u32[]{:S(2)}, u32[]{:S(2)}) collective-permute-start(bf16[2,2,2,128,512]{4,3,2,1,0:T(8,128)(2,1)} %collective-permute-done.6.refs_0_), channel_id=1, source_target_pairs={{0,16},{1,17},{2,18},{3,19},{4,20},{5,21},{6,22},{7,23},{8,24},{9,... | collective-permute-start | bytes 3145736 | tf_op jit(solution)/shard_map/ppermute | solution.py:44
  87.4 9.6 %collective-permute-start.15 = (bf16[2,2,2,128,512]{4,3,2,1,0:T(8,128)(2,1)}, bf16[2,2,2,128,512]{4,3,2,1,0:T(8,128)(2,1)S(1)}, u32[]{:S(2)}, u32[]{:S(2)}) collective-permute-start(bf16[2,2,2,128,512]{4,3,2,1,0:T(8,128)(2,1)} %collective-permute-done.7.refs_1_), channel_id=1, source_target_pairs={{0,16},{1,17},{2,18},{3,19},{4,20},{5,21},{6,22},{7,23},{8,24},{9,... | collective-permute-start | bytes 3145736 | tf_op jit(solution)/shard_map/ppermute | solution.py:44
  87.5 9.5 %collective-permute-start.16 = (bf16[2,2,2,128,512]{4,3,2,1,0:T(8,128)(2,1)S(1)}, bf16[2,2,2,128,512]{4,3,2,1,0:T(8,128)(2,1)S(1)}, u32[]{:S(2)}, u32[]{:S(2)}) collective-permute-start(bf16[2,2,2,128,512]{4,3,2,1,0:T(8,128)(2,1)S(1)} %collective-permute-done.8.refs_2_), channel_id=1, source_target_pairs={{0,16},{1,17},{2,18},{3,19},{4,20},{5,21},{6,22},{7,23},{8,24},{9,... | collective-permute-start | bytes 3145736 | tf_op jit(solution)/shard_map/ppermute | solution.py:44
  87.9 9.1 %collective-permute-start.17 = (bf16[2,2,2,128,512]{4,3,2,1,0:T(8,128)(2,1)}, bf16[2,2,2,128,512]{4,3,2,1,0:T(8,128)(2,1)S(1)}, u32[]{:S(2)}, u32[]{:S(2)}) collective-permute-start(bf16[2,2,2,128,512]{4,3,2,1,0:T(8,128)(2,1)} %collective-permute-done.9.refs_3_), channel_id=1, source_target_pairs={{0,16},{1,17},{2,18},{3,19},{4,20},{5,21},{6,22},{7,23},{8,24},{9,... | collective-permute-start | bytes 3145736 | tf_op jit(solution)/shard_map/ppermute | solution.py:44
  121.7 15.9 %all-to-all-start.3 = ((bf16[16,8,576]{2,1,0:T(8,128)(2,1)}), bf16[16,8,576]{2,1,0:T(8,128)(2,1)S(1)}, u32[]{:S(2)}, u32[]{:S(2)}) async-start(bf16[16,8,576]{2,1,0:T(8,128)(2,1)} %collect.1), calls=%async_computation.3 | async-start | bytes 327680 | tf_op jit(solution)/shard_map/prompt_return/all_to_all | solution.py:411

commit v3 on v2

--- a/solution.py
+++ b/solution.py
@@ -366,7 +366,9 @@
         near_peer = [swap(low), swap(high)]
 
     with jax.named_scope("prompt_exchange"):
-        prompt_rows = lax.all_to_all(select(prompt_of, column), "seq", 0, 0, tiled=True).reshape(prompts, WIDTH)
+        chosen = select(prompt_of, column)
+        chosen, query_nope, out_grad = lax.optimization_barrier((chosen, query_nope, out_grad))
+        prompt_rows = lax.all_to_all(chosen, "seq", 0, 0, tiled=True).reshape(prompts, WIDTH)
 
     with jax.named_scope("pair_numbers"):
         order = (0, -1, 1, 2)
@@ -395,7 +397,9 @@
         return attention(sources, scalars, q, g, query_rope, prompt_rows, latent_rows, own_bias, state, last)
 
     with jax.named_scope("weights_rest"):
-        low, high, *lead, prompt_rows = lax.optimization_barrier((low, high, *lead, prompt_rows))
+        q, g, own_bias, low, high, *lead, prompt_rows = lax.optimization_barrier(
+            (q, g, own_bias, low, high, *lead, prompt_rows)
+        )
         rest = [second_ring(high, 1), second_ring(low, -1), second_ring(lead[0], 1), second_ring(lead[1], -1)]
         lead_peer = [swap(w) for w in lead]
     state = work([low, high, *near_peer], near_pairs, None)

time: 139 us -> 139 us (level)
  starting transfers between devices: 44.1 us -> 47.7 us
  waiting for transfers between devices: 21.5 us -> 18.9 us
    unnamed x31 -> x25, local copies, waits for them, and re-layouts: 15 us -> 7.12 us
    all_to_all x1, waiting for transfers between devices: 7.67 us -> 0.56 us  [local(): lax.all_to_all(chosen, 'seq', 0, 0, tiled=True).reshape(prompts, WIDTH)]
    optimization_barrier x0 -> x2, local copies, waits for them, and re-layouts: none -> 6.98 us  [local(): lax.optimization_barrier((chosen, query_nope, out_grad))]
    all_to_all x1, starting transfers between devices: 5.44 us -> 8.96 us  [local(): sums = lax.all_to_all(collect(prompt_of, parts), 'dp', 0, 0, tiled=True)]
    ppermute x18, waiting for transfers between devices: 0.41 us -> 3.08 us  [permute(): return lax.ppermute(array, AXES, pairs)]
    all_to_all x1, waiting for transfers between devices: 8.03 us -> 9.86 us  [local(): column = lax.all_to_all(copies, 'dp', 0, 0, tiled=True)]
  transfers between devices with their start and end apart: 21 -> 21, of which waited for: 5 -> 6; matrix products, arithmetic and copies ran while one was open for 11% -> 11% of each run, Pallas kernels for 20% -> 20%
where the time goes in v3:
time: 139 us; the launch traced here: 138 us
  starting transfers between devices  47.7 us (34%)
  Pallas kernels  38.3 us (28%)
  waiting for transfers between devices  18.9 us (14%)
  local copies, waits for them, and re-layouts  14.8 us (11%)
  blocking collectives  14.5 us (10%)
  other arithmetic  2.88 us (2%)
    pallas_call x4, Pallas kernels, attention(): pl.pallas_call(functools.partial(attention_kernel, counts, first, last),...  33.3 us
    ppermute x18, starting transfers between devices, permute(): return lax.ppermute(array, AXES, pairs)  23.9 us
    all_to_all x1, blocking collectives, local(): lax.all_to_all(prompt_part.reshape(members, rows, WIDTH), 'seq', 0, 0, ti...  14.5 us
    all_to_all x1, starting transfers between devices, local(): column = lax.all_to_all(copies, 'dp', 0, 0, tiled=True)  10.6 us
    all_to_all x1, waiting for transfers between devices, local(): column = lax.all_to_all(copies, 'dp', 0, 0, tiled=True)  9.86 us
    all_to_all x1, starting transfers between devices, local(): sums = lax.all_to_all(collect(prompt_of, parts), 'dp', 0, 0, tiled=True)  8.96 us
    unnamed x25, local copies, waits for them, and re-layouts  7.12 us
    optimization_barrier x2, local copies, waits for them, and re-layouts, local(): lax.optimization_barrier((chosen, query_nope, out_grad))  6.98 us
  transfers between devices with their start and end apart: 21, of which 6 were waited for; matrix products, arithmetic and copies ran while one was open for 11% of the time, Pallas kernels for 20%

profile of v3, /device:TPU:1, one launch (start us, length us, event | category | flops | bytes accessed | tf_op | source)
XLA Modules:
  0.0 137.9 jit_solution(1900184987965433639)
XLA Ops:
  0.7 1.1 fusion
  1.7 2.5 %collective-permute-start = (bf16[2,2,128,512]{3,2,1,0:T(8,128)(2,1)S(1)}, bf16[2,2,128,512]{3,2,1,0:T(8,128)(2,1)S(1)}, u32[]{:S(2)}, u32[]{:S(2)}) collective-permute-start(bf16[2,2,128,512]{3,2,1,0:T(8,128)(2,1)S(1)} %bitcast.65), channel_id=1, source_target_pairs={{0,1},{1,2},{2,3},{3,0},{4,5},{5,6},{6,7},{7,4},{8,9},{9,10},{10,1... | collective-permute-start | bytes 1572872 | tf_op jit(solution)/shard_map/weights_first_ring/ppermute | solution.py:44
  4.3 3.1 %collective-permute-start.2 = (bf16[2,128,512]{2,1,0:T(8,128)(2,1)S(1)}, bf16[2,128,512]{2,1,0:T(8,128)(2,1)S(1)}, u32[]{:S(2)}, u32[]{:S(2)}) collective-permute-start(bf16[2,128,512]{2,1,0:T(8,128)(2,1)S(1)} %get-tuple-element.78), channel_id=1, source_target_pairs={{0,2},{1,3},{2,0},{3,1},{4,6},{5,7},{6,4},{7,5},{8,10},{9,11},{10,... | collective-permute-start | bytes 786440 | tf_op jit(solution)/shard_map/weights_first_ring/ppermute | solution.py:44
  7.4 2.2 %collective-permute-start.3 = (bf16[2,128,512]{2,1,0:T(8,128)(2,1)S(1)}, bf16[2,128,512]{2,1,0:T(8,128)(2,1)S(1)}, u32[]{:S(2)}, u32[]{:S(2)}) collective-permute-start(bf16[2,128,512]{2,1,0:T(8,128)(2,1)S(1)} %get-tuple-element.79), channel_id=1, source_target_pairs={{0,2},{1,3},{2,0},{3,1},{4,6},{5,7},{6,4},{7,5},{8,10},{9,11},{10,... | collective-permute-start | bytes 786440 | tf_op jit(solution)/shard_map/weights_first_ring/ppermute | solution.py:44
  9.6 1.1 collective-permute-start.1
  10.7 0.7 broadcast_in_dim.21
  11.4 10.6 %all-to-all-start = ((bf16[16,8,576]{2,1,0:T(8,128)(2,1)}), bf16[16,8,576]{2,1,0:T(8,128)(2,1)S(1)}, u32[]{:S(2)}, u32[]{:S(2)}) async-start(bf16[16,8,576]{2,1,0:T(8,128)(2,1)} %broadcast_in_dim.21), calls=%async_computation | async-start | bytes 327680 | tf_op jit(solution)/shard_map/prompt_gather/all_to_all | solution.py:360
  22.0 0.0 collective-permute-done.2
  22.0 0.0 collective-permute-done.3
  22.0 0.1 maximum_bitcast_fusion
  22.1 0.0 collective-permute-done
  22.1 0.0 copy-start.7
  22.1 0.1 pad_maximum_fusion.refs_0_
  22.2 0.3 collective-permute-done.1
  22.5 0.1 pad_maximum_fusion.1.refs_1_
  22.6 9.9 %all-to-all-done.rows_ref = bf16[16,8,576]{2,1,0:T(8,128)(2,1)S(1)} async-done(((bf16[16,8,576]{2,1,0:T(8,128)(2,1)}), bf16[16,8,576]{2,1,0:T(8,128)(2,1)S(1)}, u32[]{:S(2)}, u32[]{:S(2)}) %all-to-all-start) | async-done | bytes 147488 | tf_op jit(solution)/shard_map/prompt_gather/all_to_all | solution.py:360
  32.4 0.0 collective-permute-start.4
  32.4 2.7 %collective-permute-start.5 = (bf16[2,2,2,128,512]{4,3,2,1,0:T(8,128)(2,1)S(1)}, bf16[2,2,2,128,512]{4,3,2,1,0:T(8,128)(2,1)}, u32[]{:S(2)}, u32[]{:S(2)}) collective-permute-start(bf16[2,2,2,128,512]{4,3,2,1,0:T(8,128)(2,1)S(1)} %pad_maximum_fusion.1.refs_1_), channel_id=1, source_target_pairs={{0,44},{1,45},{2,46},{3,47},{4,0},{5,1},{6,2},{7,3},{8,4},{9,5},{1... | collective-permute-start | bytes 3145736 | tf_op jit(solution)/shard_map/weights_second_ring/ppermute | solution.py:44
  35.1 2.4 %select.9 = bf16[16,8,576]{2,1,0:T(8,128)(2,1)} custom-call(s32[16,16]{1,0:T(8,128)} %prompt_ref.3, bf16[16,8,576]{2,1,0:T(8,128)(2,1)} %copy-done.5), custom_call_target="tpu_custom_call" | custom-call | tf_op jit(solution)/shard_map/prompt_exchange/select/pallas_call | solution.py:300
  37.5 4.3 %all-to-all-start.1 = ((bf16[16,8,576]{2,1,0:T(8,128)(2,1)}), bf16[16,8,576]{2,1,0:T(8,128)(2,1)S(1)}, u32[]{:S(2)}, u32[]{:S(2)}) async-start(bf16[16,8,576]{2,1,0:T(8,128)(2,1)} %select.9), calls=%async_computation.1 | async-start | bytes 327680 | tf_op jit(solution)/shard_map/prompt_exchange/all_to_all | solution.py:371
  41.8 0.1 fusion.2.refs_18_
  41.9 0.0 copy-start.4
  41.9 1.7 %collective-permute-start.12 = (bf16[2,2,2,128,512]{4,3,2,1,0:T(8,128)(2,1)S(1)}, bf16[2,2,2,128,512]{4,3,2,1,0:T(8,128)(2,1)}, u32[]{:S(2)}, u32[]{:S(2)}) collective-permute-start(bf16[2,2,2,128,512]{4,3,2,1,0:T(8,128)(2,1)S(1)} %pad_maximum_fusion.refs_0_), channel_id=1, source_target_pairs={{0,16},{1,17},{2,18},{3,19},{4,20},{5,21},{6,22},{7,23},{8,24},{9,... | collective-permute-start | bytes 3145736 | tf_op jit(solution)/shard_map/weights_second_ring/ppermute | solution.py:44
  43.6 0.1 collective-permute-start.13
  43.7 4.3 %copy.44 = bf16[128,64,128]{2,0,1:T(8,128)(2,1)} copy(bf16[128,64,128]{2,1,0:T(8,128)(2,1)} %param.34) | data formatting | bytes 4194304 | tf_op jit(solution)/shard_map/prompt_exchange/optimization_barrier | solution.py:370
  47.9 2.7 %copy.45 = bf16[128,64,128]{2,0,1:T(8,128)(2,1)} copy(bf16[128,64,128]{2,1,0:T(8,128)(2,1)S(1)} %copy-done.4) | data formatting | bytes 4194304 | tf_op jit(solution)/shard_map/prompt_exchange/optimization_barrier | solution.py:370
  50.7 0.6 all-to-all-done.1
  51.2 0.0 collective-permute-done.4.refs_0_
  51.2 0.0 collective-permute-done.5.refs_1_
  51.2 4.0 %collective-permute-start.10 = (bf16[2,2,2,128,512]{4,3,2,1,0:T(8,128)(2,1)}, bf16[2,2,2,128,512]{4,3,2,1,0:T(8,128)(2,1)S(1)}, u32[]{:S(2)}, u32[]{:S(2)}) collective-permute-start(bf16[2,2,2,128,512]{4,3,2,1,0:T(8,128)(2,1)} %collective-permute-done.4.refs_0_), channel_id=1, source_target_pairs={{0,16},{1,17},{2,18},{3,19},{4,20},{5,21},{6,22},{7,23},{8,24},{9,... | collective-permute-start | bytes 3145736 | tf_op jit(solution)/shard_map/weights_rest/ppermute | solution.py:44
  55.3 0.1 collective-permute-start.11
  55.4 0.2 collective-permute-start.8
  55.6 0.0 collective-permute-done.12.refs_2_
  55.6 0.9 collective-permute-start.6
  56.4 0.0 collective-permute-done.13.refs_3_
  56.4 1.8 %collective-permute-start.7 = (bf16[2,2,2,128,512]{4,3,2,1,0:T(8,128)(2,1)S(1)}, bf16[2,2,2,128,512]{4,3,2,1,0:T(8,128)(2,1)}, u32[]{:S(2)}, u32[]{:S(2)}) collective-permute-start(bf16[2,2,2,128,512]{4,3,2,1,0:T(8,128)(2,1)S(1)} %pad_maximum_fusion.refs_0_), channel_id=1, source_target_pairs={{0,44},{1,45},{2,46},{3,47},{4,0},{5,1},{6,2},{7,3},{8,4},{9,5},{1... | collective-permute-start | bytes 3145736 | tf_op jit(solution)/shard_map/weights_rest/ppermute | solution.py:44
  58.3 0.1 collective-permute-done.10.refs_2_
  58.3 1.0 copy-done
  59.3 1.5 %collective-permute-start.9 = (bf16[2,2,2,128,512]{4,3,2,1,0:T(8,128)(2,1)}, bf16[2,2,2,128,512]{4,3,2,1,0:T(8,128)(2,1)}, u32[]{:S(2)}, u32[]{:S(2)}) collective-permute-start(bf16[2,2,2,128,512]{4,3,2,1,0:T(8,128)(2,1)} %collective-permute-done.5.refs_1_), channel_id=1, source_target_pairs={{0,44},{1,45},{2,46},{3,47},{4,0},{5,1},{6,2},{7,3},{8,4},{9,5},{1... | collective-permute-start | bytes 3145736 | tf_op jit(solution)/shard_map/weights_rest/ppermute | solution.py:44
  60.8 1.1 copy.47.refs_17_
  61.9 0.7 fusion.18
  62.6 0.1 pad_add_fusion.1.pair_ref
  62.7 0.1 pad_add_fusion.pair_ref
  62.7 7.6 %attention.4 = (f32[256,512]{1,0:T(8,128)S(1)}, f32[256,128]{1,0:T(8,128)S(1)}, bf16[32,2,128,128]{3,2,1,0:T(8,128)(2,1)}, bf16[128,4096]{1,0:T(8,128)(2,1)}) custom-call(s32[8]{0:T(128)S(1)} %pad_add_fusion.1.pair_ref, s32[16,16]{1,0:T(8,128)S(1)} %copy-done.2, s32[16]{0:T(128)S(1)} %copy-done.3, bf16[2,2,2,128,512]{4,3,2,1,0:T(8,128)(2,1)S(1)} %pad_maximum_fusion.refs_0_, ...), custom_call_target="tpu_custom_call" | custom-call | tf_op jit(solution)/shard_map/attention/pallas_call | solution.py:268
  70.4 0.0 collective-permute-done.11.refs_3_
  70.4 0.0 copy-start.8
  70.4 0.0 copy-start.9
  70.4 9.0 %attention.5 = (f32[256,512]{1,0:T(8,128)S(1)}, f32[256,128]{1,0:T(8,128)S(1)}, bf16[32,2,128,128]{3,2,1,0:T(8,128)(2,1)}, bf16[128,4096]{1,0:T(8,128)(2,1)}) custom-call(s32[8]{0:T(128)S(1)} %pad_add_fusion.pair_ref, s32[16,16]{1,0:T(8,128)S(1)} %copy-done.2, s32[16]{0:T(128)S(1)} %copy-done.3, ...), custom_call_target="tpu_custom_call", output_to_operand_aliasing={{2}: (24, {}), {3}: (25, {})} | custom-call | tf_op jit(solution)/shard_map/attention/pallas_call | solution.py:268
  79.4 2.7 %collective-permute-done.6.refs_0_ = bf16[2,2,2,128,512]{4,3,2,1,0:T(8,128)(2,1)} collective-permute-done((bf16[2,2,2,128,512]{4,3,2,1,0:T(8,128)(2,1)S(1)}, bf16[2,2,2,128,512]{4,3,2,1,0:T(8,128)(2,1)}, u32[]{:S(2)}, u32[]{:S(2)}) %collective-permute-start.6) | collective-permute-done | bytes 1048608 | tf_op jit(solution)/shard_map/weights_rest/ppermute | solution.py:44
  82.1 0.0 collective-permute-done.7.refs_1_
  82.1 1.4 %collective-permute-start.14 = (bf16[2,2,2,128,512]{4,3,2,1,0:T(8,128)(2,1)}, bf16[2,2,2,128,512]{4,3,2,1,0:T(8,128)(2,1)S(1)}, u32[]{:S(2)}, u32[]{:S(2)}) collective-permute-start(bf16[2,2,2,128,512]{4,3,2,1,0:T(8,128)(2,1)} %collective-permute-done.6.refs_0_), channel_id=1, source_target_pairs={{0,16},{1,17},{2,18},{3,19},{4,20},{5,21},{6,22},{7,23},{8,24},{9,... | collective-permute-start | bytes 3145736 | tf_op jit(solution)/shard_map/ppermute | solution.py:44
  83.5 0.1 collective-permute-start.15
  83.6 0.4 collective-permute-start.16
  84.0 0.1 collective-permute-start.17
  84.1 9.0 %attention.6 = (f32[256,512]{1,0:T(8,128)S(1)}, f32[256,128]{1,0:T(8,128)S(1)}, bf16[32,2,128,128]{3,2,1,0:T(8,128)(2,1)}, bf16[128,4096]{1,0:T(8,128)(2,1)}) custom-call(s32[8]{0:T(128)S(1)} %get-tuple-element.80.pair_ref, s32[16,16]{1,0:T(8,128)S(1)} %copy-done.2, s32[16]{0:T(128)S(1)} %copy-done.3, ...), custom_call_target="tpu_custom_call", output_to_operand_aliasing={{2}: (24, {}), {3}: (25, {})} | custom-call | tf_op jit(solution)/shard_map/attention/pallas_call | solution.py:268
  93.1 0.0 collective-permute-done.15.refs_1_
  93.1 7.8 %attention.7 = (f32[128,576]{1,0:T(8,128)S(1)}, bf16[128,576]{1,0:T(8,128)(2,1)S(1)}, bf16[32,2,128,128]{3,2,1,0:T(8,128)(2,1)}, bf16[128,4096]{1,0:T(8,128)(2,1)}) custom-call(s32[8]{0:T(128)S(1)} %get-tuple-element.81.pair_ref, s32[16,16]{1,0:T(8,128)S(1)} %copy-done.2, s32[16]{0:T(128)S(1)} %copy-done.3, ...), custom_call_target="tpu_custom_call", output_to_operand_aliasing={{2}: (24, {}), {3}: (25, {})} | custom-call | tf_op jit(solution)/shard_map/attention/pallas_call | solution.py:268
  100.9 14.5 %all_to_all.20.parts_ref = f32[16,8,576]{2,1,0:T(8,128)} all-to-all(f32[16,8,576]{2,1,0:T(8,128)S(1)} %bitcast.31), channel_id=1, replica_groups=mesh['dp'=16,'seq'=16] {'seq'}, dimensions={0} | all-to-all | bytes 589824 | tf_op jit(solution)/shard_map/prompt_return/all_to_all | solution.py:414
  115.4 2.5 %collect.1 = bf16[16,8,576]{2,1,0:T(8,128)(2,1)} custom-call(s32[16,16]{1,0:T(8,128)} %prompt_ref.3, f32[16,8,576]{2,1,0:T(8,128)} %all_to_all.20.parts_ref), custom_call_target="tpu_custom_call" | custom-call | tf_op jit(solution)/shard_map/prompt_return/collect/pallas_call | solution.py:300
  117.9 9.0 %all-to-all-start.3 = ((bf16[16,8,576]{2,1,0:T(8,128)(2,1)}), bf16[16,8,576]{2,1,0:T(8,128)(2,1)S(1)}, u32[]{:S(2)}, u32[]{:S(2)}) async-start(bf16[16,8,576]{2,1,0:T(8,128)(2,1)} %collect.1), calls=%async_computation.3 | async-start | bytes 327680 | tf_op jit(solution)/shard_map/prompt_return/all_to_all | solution.py:415
  126.9 4.3 %copy.50 = bf16[128,64,128]{2,1,0:T(8,128)(2,1)} copy(bf16[128,64,128]{2,0,1:T(8,128)(2,1)} %bitcast.64) | data formatting | bytes 4194304
  131.1 0.8 copy.51
  131.9 5.4 %all-to-all-done.3 = bf16[16,8,576]{2,1,0:T(8,128)(2,1)S(1)} async-done(((bf16[16,8,576]{2,1,0:T(8,128)(2,1)}), bf16[16,8,576]{2,1,0:T(8,128)(2,1)S(1)}, u32[]{:S(2)}, u32[]{:S(2)}) %all-to-all-start.3) | async-done | bytes 147488 | tf_op jit(solution)/shard_map/prompt_return/all_to_all | solution.py:415
  137.3 0.6 convert_reduce_fusion
  (24 shorter events, 0.1 us)
Async XLA Ops:
  0.6 10.1 %copy-start.6 = (bf16[1,8,576]{2,1,0:T(8,128)(2,1)S(1)}, bf16[1,8,576]{2,1,0:T(8,128)(2,1)}, u32[]{:S(2)}) copy-start(bf16[1,8,576]{2,1,0:T(8,128)(2,1)} %param.38) | copy-start | bytes 27652
  1.7 20.3 %collective-permute-start = (bf16[2,2,128,512]{3,2,1,0:T(8,128)(2,1)S(1)}, bf16[2,2,128,512]{3,2,1,0:T(8,128)(2,1)S(1)}, u32[]{:S(2)}, u32[]{:S(2)}) collective-permute-start(bf16[2,2,128,512]{3,2,1,0:T(8,128)(2,1)S(1)} %bitcast.65), channel_id=1, source_target_pairs={{0,1},{1,2},{2,3},{3,0},{4,5},{5,6},{6,7},{7,4},{8,9},{9,10},{10,1... | collective-permute-start | bytes 1572872 | tf_op jit(solution)/shard_map/weights_first_ring/ppermute | solution.py:44
  4.3 17.7 %collective-permute-start.2 = (bf16[2,128,512]{2,1,0:T(8,128)(2,1)S(1)}, bf16[2,128,512]{2,1,0:T(8,128)(2,1)S(1)}, u32[]{:S(2)}, u32[]{:S(2)}) collective-permute-start(bf16[2,128,512]{2,1,0:T(8,128)(2,1)S(1)} %get-tuple-element.78), channel_id=1, source_target_pairs={{0,2},{1,3},{2,0},{3,1},{4,6},{5,7},{6,4},{7,5},{8,10},{9,11},{10,... | collective-permute-start | bytes 786440 | tf_op jit(solution)/shard_map/weights_first_ring/ppermute | solution.py:44
  7.4 14.6 %collective-permute-start.3 = (bf16[2,128,512]{2,1,0:T(8,128)(2,1)S(1)}, bf16[2,128,512]{2,1,0:T(8,128)(2,1)S(1)}, u32[]{:S(2)}, u32[]{:S(2)}) collective-permute-start(bf16[2,128,512]{2,1,0:T(8,128)(2,1)S(1)} %get-tuple-element.79), channel_id=1, source_target_pairs={{0,2},{1,3},{2,0},{3,1},{4,6},{5,7},{6,4},{7,5},{8,10},{9,11},{10,... | collective-permute-start | bytes 786440 | tf_op jit(solution)/shard_map/weights_first_ring/ppermute | solution.py:44
  9.6 12.9 %collective-permute-start.1 = (bf16[2,2,128,512]{3,2,1,0:T(8,128)(2,1)S(1)}, bf16[2,2,128,512]{3,2,1,0:T(8,128)(2,1)S(1)}, u32[]{:S(2)}, u32[]{:S(2)}) collective-permute-start(bf16[2,2,128,512]{3,2,1,0:T(8,128)(2,1)S(1)} %bitcast.66), channel_id=1, source_target_pairs={{0,3},{1,0},{2,1},{3,2},{4,7},{5,4},{6,5},{7,6},{8,11},{9,8},{10,9... | collective-permute-start | bytes 1572872 | tf_op jit(solution)/shard_map/weights_first_ring/ppermute | solution.py:44
  11.4 21.0 %all-to-all-start = ((bf16[16,8,576]{2,1,0:T(8,128)(2,1)}), bf16[16,8,576]{2,1,0:T(8,128)(2,1)S(1)}, u32[]{:S(2)}, u32[]{:S(2)}) async-start(bf16[16,8,576]{2,1,0:T(8,128)(2,1)} %broadcast_in_dim.21), calls=%async_computation | async-start | bytes 327680 | tf_op jit(solution)/shard_map/prompt_gather/all_to_all | solution.py:360
  22.1 19.7 %copy-start.7 = (s32[1,128]{1,0:T(1,128)S(1)}, s32[1,128]{1,0:T(1,128)}, u32[]{:S(2)}) copy-start(s32[1,128]{1,0:T(1,128)} %param.43) | copy-start | bytes 1540
  32.4 2.7 %copy-start.5 = (bf16[16,8,576]{2,1,0:T(8,128)(2,1)}, bf16[16,8,576]{2,1,0:T(8,128)(2,1)S(1)}, u32[]{:S(2)}) copy-start(bf16[16,8,576]{2,1,0:T(8,128)(2,1)S(1)} %all-to-all-done.rows_ref) | copy-start | bytes 442372
  32.4 18.8 %collective-permute-start.4 = (bf16[2,2,2,128,512]{4,3,2,1,0:T(8,128)(2,1)S(1)}, bf16[2,2,2,128,512]{4,3,2,1,0:T(8,128)(2,1)}, u32[]{:S(2)}, u32[]{:S(2)}) collective-permute-start(bf16[2,2,2,128,512]{4,3,2,1,0:T(8,128)(2,1)S(1)} %pad_maximum_fusion.refs_0_), channel_id=1, source_target_pairs={{0,4},{1,5},{2,6},{3,7},{4,8},{5,9},{6,10},{7,11},{8,12},{9,13},{1... | collective-permute-start | bytes 3145736 | tf_op jit(solution)/shard_map/weights_second_ring/ppermute | solution.py:44
  32.4 18.8 %collective-permute-start.5 = (bf16[2,2,2,128,512]{4,3,2,1,0:T(8,128)(2,1)S(1)}, bf16[2,2,2,128,512]{4,3,2,1,0:T(8,128)(2,1)}, u32[]{:S(2)}, u32[]{:S(2)}) collective-permute-start(bf16[2,2,2,128,512]{4,3,2,1,0:T(8,128)(2,1)S(1)} %pad_maximum_fusion.1.refs_1_), channel_id=1, source_target_pairs={{0,44},{1,45},{2,46},{3,47},{4,0},{5,1},{6,2},{7,3},{8,4},{9,5},{1... | collective-permute-start | bytes 3145736 | tf_op jit(solution)/shard_map/weights_second_ring/ppermute | solution.py:44
  37.5 13.7 %all-to-all-start.1 = ((bf16[16,8,576]{2,1,0:T(8,128)(2,1)}), bf16[16,8,576]{2,1,0:T(8,128)(2,1)S(1)}, u32[]{:S(2)}, u32[]{:S(2)}) async-start(bf16[16,8,576]{2,1,0:T(8,128)(2,1)} %select.9), calls=%async_computation.1 | async-start | bytes 327680 | tf_op jit(solution)/shard_map/prompt_exchange/all_to_all | solution.py:371
  41.9 6.0 %copy-start.4 = (bf16[128,64,128]{2,1,0:T(8,128)(2,1)S(1)}, bf16[128,64,128]{2,1,0:T(8,128)(2,1)}, u32[]{:S(2)}) copy-start(bf16[128,64,128]{2,1,0:T(8,128)(2,1)} %param.36) | copy-start | bytes 6291460
  41.9 13.7 %collective-permute-start.12 = (bf16[2,2,2,128,512]{4,3,2,1,0:T(8,128)(2,1)S(1)}, bf16[2,2,2,128,512]{4,3,2,1,0:T(8,128)(2,1)}, u32[]{:S(2)}, u32[]{:S(2)}) collective-permute-start(bf16[2,2,2,128,512]{4,3,2,1,0:T(8,128)(2,1)S(1)} %pad_maximum_fusion.refs_0_), channel_id=1, source_target_pairs={{0,16},{1,17},{2,18},{3,19},{4,20},{5,21},{6,22},{7,23},{8,24},{9,... | collective-permute-start | bytes 3145736 | tf_op jit(solution)/shard_map/weights_second_ring/ppermute | solution.py:44
  43.6 12.9 %collective-permute-start.13 = (bf16[2,2,2,128,512]{4,3,2,1,0:T(8,128)(2,1)S(1)}, bf16[2,2,2,128,512]{4,3,2,1,0:T(8,128)(2,1)}, u32[]{:S(2)}, u32[]{:S(2)}) collective-permute-start(bf16[2,2,2,128,512]{4,3,2,1,0:T(8,128)(2,1)S(1)} %pad_maximum_fusion.1.refs_1_), channel_id=1, source_target_pairs={{0,16},{1,17},{2,18},{3,19},{4,20},{5,21},{6,22},{7,23},{8,24},{9,... | collective-permute-start | bytes 3145736 | tf_op jit(solution)/shard_map/weights_second_ring/ppermute | solution.py:44
  47.9 14.0 %copy-start.10 = (s32[4]{0:T(128)S(1)}, s32[4]{0:T(128)}, u32[]{:S(2)}) copy-start(s32[4]{0:T(128)} %constant.67.clone) | copy-start | bytes 52
  47.9 14.8 %copy-start.2 = (s32[16,16]{1,0:T(8,128)S(1)}, s32[16,16]{1,0:T(8,128)}, u32[]{:S(2)}) copy-start(s32[16,16]{1,0:T(8,128)} %prompt_ref.3) | copy-start | bytes 3076
  47.9 14.8 %copy-start.3 = (s32[16]{0:T(128)S(1)}, s32[16]{0:T(128)}, u32[]{:S(2)}) copy-start(s32[16]{0:T(128)} %prompt_len_ref.7) | copy-start | bytes 196
  51.2 7.1 %collective-permute-start.10 = (bf16[2,2,2,128,512]{4,3,2,1,0:T(8,128)(2,1)}, bf16[2,2,2,128,512]{4,3,2,1,0:T(8,128)(2,1)S(1)}, u32[]{:S(2)}, u32[]{:S(2)}) collective-permute-start(bf16[2,2,2,128,512]{4,3,2,1,0:T(8,128)(2,1)} %collective-permute-done.4.refs_0_), channel_id=1, source_target_pairs={{0,16},{1,17},{2,18},{3,19},{4,20},{5,21},{6,22},{7,23},{8,24},{9,... | collective-permute-start | bytes 3145736 | tf_op jit(solution)/shard_map/weights_rest/ppermute | solution.py:44
  55.3 15.1 %collective-permute-start.11 = (bf16[2,2,2,128,512]{4,3,2,1,0:T(8,128)(2,1)}, bf16[2,2,2,128,512]{4,3,2,1,0:T(8,128)(2,1)}, u32[]{:S(2)}, u32[]{:S(2)}) collective-permute-start(bf16[2,2,2,128,512]{4,3,2,1,0:T(8,128)(2,1)} %collective-permute-done.5.refs_1_), channel_id=1, source_target_pairs={{0,16},{1,17},{2,18},{3,19},{4,20},{5,21},{6,22},{7,23},{8,24},{9,... | collective-permute-start | bytes 3145736 | tf_op jit(solution)/shard_map/weights_rest/ppermute | solution.py:44
  55.4 26.7 %collective-permute-start.8 = (bf16[2,2,2,128,512]{4,3,2,1,0:T(8,128)(2,1)}, bf16[2,2,2,128,512]{4,3,2,1,0:T(8,128)(2,1)S(1)}, u32[]{:S(2)}, u32[]{:S(2)}) collective-permute-start(bf16[2,2,2,128,512]{4,3,2,1,0:T(8,128)(2,1)} %collective-permute-done.4.refs_0_), channel_id=1, source_target_pairs={{0,4},{1,5},{2,6},{3,7},{4,8},{5,9},{6,10},{7,11},{8,12},{9,13},{1... | collective-permute-start | bytes 3145736 | tf_op jit(solution)/shard_map/weights_rest/ppermute | solution.py:44
  55.6 26.5 %collective-permute-start.6 = (bf16[2,2,2,128,512]{4,3,2,1,0:T(8,128)(2,1)S(1)}, bf16[2,2,2,128,512]{4,3,2,1,0:T(8,128)(2,1)}, u32[]{:S(2)}, u32[]{:S(2)}) collective-permute-start(bf16[2,2,2,128,512]{4,3,2,1,0:T(8,128)(2,1)S(1)} %pad_maximum_fusion.1.refs_1_), channel_id=1, source_target_pairs={{0,4},{1,5},{2,6},{3,7},{4,8},{5,9},{6,10},{7,11},{8,12},{9,13},{1... | collective-permute-start | bytes 3145736 | tf_op jit(solution)/shard_map/weights_rest/ppermute | solution.py:44
  56.4 25.6 %collective-permute-start.7 = (bf16[2,2,2,128,512]{4,3,2,1,0:T(8,128)(2,1)S(1)}, bf16[2,2,2,128,512]{4,3,2,1,0:T(8,128)(2,1)}, u32[]{:S(2)}, u32[]{:S(2)}) collective-permute-start(bf16[2,2,2,128,512]{4,3,2,1,0:T(8,128)(2,1)S(1)} %pad_maximum_fusion.refs_0_), channel_id=1, source_target_pairs={{0,44},{1,45},{2,46},{3,47},{4,0},{5,1},{6,2},{7,3},{8,4},{9,5},{1... | collective-permute-start | bytes 3145736 | tf_op jit(solution)/shard_map/weights_rest/ppermute | solution.py:44
  58.3 1.0 copy-start
  59.3 22.8 %collective-permute-start.9 = (bf16[2,2,2,128,512]{4,3,2,1,0:T(8,128)(2,1)}, bf16[2,2,2,128,512]{4,3,2,1,0:T(8,128)(2,1)}, u32[]{:S(2)}, u32[]{:S(2)}) collective-permute-start(bf16[2,2,2,128,512]{4,3,2,1,0:T(8,128)(2,1)} %collective-permute-done.5.refs_1_), channel_id=1, source_target_pairs={{0,44},{1,45},{2,46},{3,47},{4,0},{5,1},{6,2},{7,3},{8,4},{9,5},{1... | collective-permute-start | bytes 3145736 | tf_op jit(solution)/shard_map/weights_rest/ppermute | solution.py:44
  62.7 7.7 %copy-start.1 = (bf16[2,2,2,128,512]{4,3,2,1,0:T(8,128)(2,1)S(1)}, bf16[2,2,2,128,512]{4,3,2,1,0:T(8,128)(2,1)}, u32[]{:S(2)}) copy-start(bf16[2,2,2,128,512]{4,3,2,1,0:T(8,128)(2,1)} %copy-done) | copy-start | bytes 3145732
  70.4 13.7 %copy-start.8 = (s32[8]{0:T(128)S(1)}, s32[8]{0:T(128)}, u32[]{:S(2)}) copy-start(s32[8]{0:T(128)} %constant.70.clone) | copy-start | bytes 100
  70.4 13.7 %copy-start.9 = (s32[8]{0:T(128)S(1)}, s32[8]{0:T(128)}, u32[]{:S(2)}) copy-start(s32[8]{0:T(128)} %constant.71.clone) | copy-start | bytes 100
  82.1 11.0 %collective-permute-start.14 = (bf16[2,2,2,128,512]{4,3,2,1,0:T(8,128)(2,1)}, bf16[2,2,2,128,512]{4,3,2,1,0:T(8,128)(2,1)S(1)}, u32[]{:S(2)}, u32[]{:S(2)}) collective-permute-start(bf16[2,2,2,128,512]{4,3,2,1,0:T(8,128)(2,1)} %collective-permute-done.6.refs_0_), channel_id=1, source_target_pairs={{0,16},{1,17},{2,18},{3,19},{4,20},{5,21},{6,22},{7,23},{8,24},{9,... | collective-permute-start | bytes 3145736 | tf_op jit(solution)/shard_map/ppermute | solution.py:44
  83.5 9.6 %collective-permute-start.15 = (bf16[2,2,2,128,512]{4,3,2,1,0:T(8,128)(2,1)}, bf16[2,2,2,128,512]{4,3,2,1,0:T(8,128)(2,1)S(1)}, u32[]{:S(2)}, u32[]{:S(2)}) collective-permute-start(bf16[2,2,2,128,512]{4,3,2,1,0:T(8,128)(2,1)} %collective-permute-done.7.refs_1_), channel_id=1, source_target_pairs={{0,16},{1,17},{2,18},{3,19},{4,20},{5,21},{6,22},{7,23},{8,24},{9,... | collective-permute-start | bytes 3145736 | tf_op jit(solution)/shard_map/ppermute | solution.py:44
  83.6 9.5 %collective-permute-start.16 = (bf16[2,2,2,128,512]{4,3,2,1,0:T(8,128)(2,1)S(1)}, bf16[2,2,2,128,512]{4,3,2,1,0:T(8,128)(2,1)S(1)}, u32[]{:S(2)}, u32[]{:S(2)}) collective-permute-start(bf16[2,2,2,128,512]{4,3,2,1,0:T(8,128)(2,1)S(1)} %collective-permute-done.8.refs_2_), channel_id=1, source_target_pairs={{0,16},{1,17},{2,18},{3,19},{4,20},{5,21},{6,22},{7,23},{8,24},{9,... | collective-permute-start | bytes 3145736 | tf_op jit(solution)/shard_map/ppermute | solution.py:44
  84.0 9.1 %collective-permute-start.17 = (bf16[2,2,2,128,512]{4,3,2,1,0:T(8,128)(2,1)}, bf16[2,2,2,128,512]{4,3,2,1,0:T(8,128)(2,1)S(1)}, u32[]{:S(2)}, u32[]{:S(2)}) collective-permute-start(bf16[2,2,2,128,512]{4,3,2,1,0:T(8,128)(2,1)} %collective-permute-done.9.refs_3_), channel_id=1, source_target_pairs={{0,16},{1,17},{2,18},{3,19},{4,20},{5,21},{6,22},{7,23},{8,24},{9,... | collective-permute-start | bytes 3145736 | tf_op jit(solution)/shard_map/ppermute | solution.py:44
  117.9 19.4 %all-to-all-start.3 = ((bf16[16,8,576]{2,1,0:T(8,128)(2,1)}), bf16[16,8,576]{2,1,0:T(8,128)(2,1)S(1)}, u32[]{:S(2)}, u32[]{:S(2)}) async-start(bf16[16,8,576]{2,1,0:T(8,128)(2,1)} %collect.1), calls=%async_computation.3 | async-start | bytes 327680 | tf_op jit(solution)/shard_map/prompt_return/all_to_all | solution.py:415
